TPU v7x, 128 devices: a whole 4x4x4 slice. The times are simulated.
128 devices in a mesh: row: 8 (over z, core), col: 16 (over y, x).
Axes of the slice: x: 4, y: 4, z: 4, core: 2. Of those that a mesh axis runs over, the one named last changes fastest.
Arguments:
- children: bfloat16 [16384, 8192], P('row', 'col'), as said below
- child_maps: int32 [2, 64], replicated, may hold values from 0 to 127, as said below
- pattern: int32 [128, 128], replicated, may hold values from 0 to 1, as said below
- own_cols: bfloat16 [16384, 1024], P('row'), as said below
Outputs:
- updated_front: bfloat16 [16384, 16384], P('row', 'col')
- factor: float32 [16384, 1024], P(('row', 'col'))
Inputs may be any that keep to these rules, and one draw needn't show every extreme that they name: Each row of child_maps is injective. For each child and each a, of the 16 entries with indices a * 16 to (a + 1) * 16 - 1, exactly 2 lie in each range p * 16 to (p + 1) * 16 - 1. For each b, the 4 entries with indices b * 4 to (b + 1) * 4 - 1 lie in different ranges q * 8 to (q + 1) * 8 - 1. `pattern`: Symmetric; 1 on the diagonal, in every tile whose two indices are both below 8, and in every tile whose two indices are both in one child's map. `children`: each child's 8192 x 8192 block is symmetric. `own_cols`: rows 0 to 1023 form a symmetric matrix whose off-diagonal entries lie in [-3, 3] and whose diagonal entries lie between 4.5 * sqrt(1024) and 6.75 * sqrt(1024); added to the children's entries assembled there, it is positive definite.
All inputs are finite; a program needn't handle non-finite values.
Results may differ from a plain program's by a relative error of at most 0.001.
Values may be sent and summed in bfloat16 or wider, within the bound.
No kernel may reach another device: no remote copies, remote signals or barrier semaphores. Data moves between devices by JAX's collectives and lax.ppermute only.
A program may use at most 128 MiB of HBM per device.

v0:
```python
import jax
import jax.numpy as jnp
from jax import lax
from jax.experimental import pallas as pl
from jax.experimental.pallas import tpu as pltpu
from jax.sharding import Mesh, PartitionSpec as P

F32 = jnp.float32
BF16 = jnp.bfloat16
I32 = jnp.int32
T = 128
PW = 512
ROW = ("z", "core")
COL = ("y", "x")
ALL = ROW + COL
FIRST = [(i, j) for i in range(4) for j in range(i + 1)]
LOWER = FIRST + [(i, j) for i in range(4, 8) for j in range(i + 1)]
HI = lax.Precision.HIGHEST
MIB = 2**20
VMEM = 56 * MIB


def nt(a, b, precision=None):
    return lax.dot_general(
        a, b, (((1,), (1,)), ((), ())), precision=precision, preferred_element_type=F32
    )


def nn(a, b, precision=None):
    return lax.dot_general(
        a, b, (((1,), (0,)), ((), ())), precision=precision, preferred_element_type=F32
    )


def halves(x):
    high = x.astype(BF16)
    return high, (x - high.astype(F32)).astype(BF16)


def nt3(a_high, a_low, b_high, b_low):
    return nt(a_high, b_high) + (nt(a_high, b_low) + nt(a_low, b_high))


def lanes(x, j):
    return jnp.broadcast_to(x[:, j : j + 1], x.shape)


def subs(x, i):
    return jnp.broadcast_to(x[i : i + 1, :], x.shape)


def rsqrt(d):
    r = lax.rsqrt(d)
    return r * (1.5 - 0.5 * d * r * r)


def invert_block(load, store):
    rest = [load(s) for s in range(16)]
    sub = lax.broadcasted_iota(I32, (8, T), 0)
    lane = lax.broadcasted_iota(I32, (8, T), 1)
    right = [(lane == sub + 8 * s).astype(F32) for s in range(16)]
    for s in range(16):
        col = [lanes(rest[s], 8 * s + t) for t in range(8)]
        a = {(i, t): subs(col[t], i) for t in range(8) for i in range(t, 8)}
        rs = []
        for t in range(8):
            rs.append(rsqrt(a[t, t]))
            for i in range(t + 1, 8):
                a[i, t] = a[i, t] * rs[t]
            for m in range(t + 1, 8):
                for i in range(m, 8):
                    a[i, m] = a[i, m] - a[i, t] * a[m, t]
        u, w = [], []
        for t in range(8):
            x, y = subs(rest[s], t), subs(right[s], t)
            for m in range(t):
                x = x - a[t, m] * u[m]
                y = y - a[t, m] * w[m]
            u.append(x * rs[t])
            w.append(y * rs[t])
        out = w[0]
        for t in range(1, 8):
            out = jnp.where(sub == t, w[t], out)
        store(s, out)
        for n in range(s + 1, 16):
            c = []
            for t in range(8):
                x = lanes(rest[n], 8 * s + t)
                for m in range(t):
                    x = x - a[t, m] * c[m]
                c.append(x * rs[t])
            x, y = rest[n], right[n]
            for t in range(8):
                x = x - c[t] * u[t]
                y = y - c[t] * w[t]
            rest[n], right[n] = x, y


def factor_panel(a, inv, out):
    out[...] = jnp.zeros((PW, PW), F32)

    def step(k, _):
        kk = pl.multiple_of(k * T, T)

        def load(s):
            return a[pl.ds(kk + 8 * s, 8), pl.ds(kk, T)]

        def store(s, v):
            inv[8 * s : 8 * s + 8, :] = v

        invert_block(load, store)
        for b in range(4):

            @pl.when(k == b)
            def _():
                lo, top = T * b, T * (b + 1)
                v = inv[...]
                if b:
                    out[lo:top, :lo] = nn(v, out[lo:top, :lo], HI)
                out[lo:top, lo:top] = v
                if b < 3:
                    col = nt(a[top:, lo:top], v, HI)
                    for j in range(b + 1, 4):
                        r = T * j
                        a[r:, r : r + T] -= nt(col[r - top :], col[r - top : r - top + T], HI)
                    out[top:, :top] -= nn(col, out[lo:top, :top], HI)

        return 0

    lax.fori_loop(0, 4, step, 0)


def panel1_kernel(lead_ref, i1_ref, i1h, i1l, a, inv):
    for n, (i, j) in enumerate(FIRST):
        a[i * T : i * T + T, j * T : j * T + T] = lead_ref[n]
    factor_panel(a, inv, i1_ref)
    i1h[...], i1l[...] = halves(i1_ref[...].T)


def panel2_kernel(lead_ref, i1_ref, lh, ll, i2h, i2l, a, low, inv, i2):
    for n, (i, j) in enumerate(LOWER):
        if i < 4:
            continue
        if j < 4:
            low[i * T - PW : i * T - PW + T, j * T : j * T + T] = lead_ref[n]
        else:
            a[i * T - PW : i * T - PW + T, j * T - PW : j * T - PW + T] = lead_ref[n]
    col = nt(low[...], i1_ref[...], HI)
    lh[...], ll[...] = halves(col.T)
    for j in range(4):
        r = T * j
        a[r:, r : r + T] -= nt(col[r:], col[r : r + T], HI)
    factor_panel(a, inv, i2)
    i2h[...], i2l[...] = halves(i2[...].T)


def panel_call(kernel, name, tiles, outs, scratch, lead, *args):
    whole = pl.BlockSpec((PW, PW), lambda i: (0, 0), pipeline_mode=pl.Buffered(1))
    return pl.pallas_call(
        kernel,
        out_shape=tuple(jax.ShapeDtypeStruct((PW, PW), t) for t in outs),
        grid=(1,),
        in_specs=[pl.BlockSpec((tiles, T, T), lambda i: (0, 0, 0), pipeline_mode=pl.Buffered(1))]
        + [whole] * len(args),
        out_specs=[whole] * len(outs),
        scratch_shapes=[pltpu.VMEM(x, F32) for x in scratch],
        compiler_params=pltpu.CompilerParams(vmem_limit_bytes=24 * MIB),
        cost_estimate=pl.CostEstimate(flops=25 * 10**9, bytes_accessed=4 * MIB, transcendentals=0),
        name=name,
    )(lead, *args)


def pack_rows_kernel(tab, top, low, out):
    for t, ref in enumerate((top, low)):
        for h in range(2):
            for k in range(4):
                out[t * 2 + h, k] = ref[64 * h : 64 * h + 64, k * T : k * T + T]


def pack_rows(children, order):
    return pl.pallas_call(
        pack_rows_kernel,
        out_shape=jax.ShapeDtypeStruct((32, 4, 64, T), BF16),
        grid_spec=pltpu.PrefetchScalarGridSpec(
            num_scalar_prefetch=1,
            grid=(8,),
            in_specs=[
                pl.BlockSpec((T, PW), lambda p, tab: (tab[2 * p], 0)),
                pl.BlockSpec((T, PW), lambda p, tab: (tab[2 * p + 1], 0)),
            ],
            out_specs=pl.BlockSpec((4, 4, 64, T), lambda p, tab: (p, 0, 0, 0)),
        ),
        compiler_params=pltpu.CompilerParams(vmem_limit_bytes=16 * MIB),
        cost_estimate=pl.CostEstimate(flops=0, bytes_accessed=4 * MIB, transcendentals=0),
        name="pack_rows",
    )(order, children, children)


def pack_columns_kernel(tab, ref, out):
    p = pl.program_id(0)
    for g in range(8):
        for s in range(2):
            part = ref[g * 16 + tab[g // 4 * 16 + p * 2 + s]]
            for q in range(2):
                out[q, g, s] = part


def pack_columns(halves_here, orders):
    return pl.pallas_call(
        pack_columns_kernel,
        out_shape=jax.ShapeDtypeStruct((16, 8, 2, 64, T), BF16),
        grid_spec=pltpu.PrefetchScalarGridSpec(
            num_scalar_prefetch=1,
            grid=(8,),
            in_specs=[
                pl.BlockSpec((128, 64, T), lambda p, tab: (0, 0, 0), pipeline_mode=pl.Buffered(1))
            ],
            out_specs=pl.BlockSpec((2, 8, 2, 64, T), lambda p, tab: (p, 0, 0, 0, 0)),
        ),
        compiler_params=pltpu.CompilerParams(vmem_limit_bytes=16 * MIB),
        cost_estimate=pl.CostEstimate(flops=0, bytes_accessed=6 * MIB, transcendentals=0),
        name="pack_columns",
    )(orders, halves_here)


TM = 512
SUB = 128
QS = 1024 // TM
RS = 2048 // TM
G = TM // T
STEPS = QS + RS
F_ROW, F_COL, F_PAT, F_AT, F_SHARE = 0, 48, 80, 272, 296


def nn3(a_high, a_low, b_high, b_low):
    return nn(jnp.concatenate([a_high, a_high, a_low], axis=1), jnp.concatenate([b_high, b_low, b_high], axis=0))


def factor_kernel(
    tab, own_q, own_r, buf_q, buf_r, i1h, i1l, lh, ll, i2h, i2l, high, low, fac, sh, sl, rest, tiles, sem
):
    step = pl.program_id(0)

    def load(n):
        ref = (buf_q.at[:, pl.ds(0, 32)], buf_r)[n]
        return pltpu.make_async_copy(ref, tiles.at[pl.ds(8 * n, 8)], sem.at[n])

    def assemble(i, slot, g):
        side = (i >= QS).astype(I32)
        stride = jnp.where(side == 1, 16, 1)
        n = i * G + g
        for j in range(8):
            kept = tab[F_PAT + n * 8 + j] != 0
            at = [(tab[F_ROW + n * 2 + c], tab[F_COL + side * 16 + c * 8 + j]) for c in range(2)]
            valid = [jnp.logical_and(a >= 0, b >= 0) for a, b in at]
            at = [side * 256 + a + b for a, b in at]
            for h in range(2):
                line = slice(g * T + 64 * h, g * T + 64 * h + 64)
                x = jnp.where(side == 1, own_r[line, j * T : j * T + T], own_q[g, j * 2 + h])
                x = jnp.where(kept, x, jnp.zeros_like(x)).astype(F32)
                for c in range(2):
                    half = jnp.where(valid[c], at[c] + h * stride, 512)
                    x = x + tiles[half // 32, half % 32].astype(F32)
                if j < 4:
                    place = slice(j * T, j * T + T)
                    sh[slot, line, place], sl[slot, line, place] = halves(x)
                else:
                    rest[slot, line, j * T - PW : j * T - PW + T] = x

    def by_inverse(xh, xl, ih, il):
        left = nn3(xh[:, :256], xl[:, :256], ih[:256, :256], il[:256, :256])
        right = nn3(xh, xl, ih[:, 256:], il[:, 256:])
        return jnp.concatenate([left, right], axis=1)

    def multiply(i, slot, between):
        count, lines = TM // SUB, SUB // T
        zero = jnp.zeros((T, PW), BF16)
        at = [slice(c * SUB, c * SUB + SUB) for c in range(count)]
        f0 = [by_inverse(sh[slot, x], sl[slot, x], i1h, i1l) for x in at]
        between(0)
        ups, f1 = [], []
        for c in range(count):
            f0h, f0l = halves(f0[c])
            ups.append(nn3(f0h, f0l, lh[...], ll[...]))
            for g in range(lines):
                first = tab[F_AT + i * G + c * lines + g]
                line, to = slice(g * T, g * T + T), slice(c * SUB + g * T, c * SUB + g * T + T)
                high[to, :PW] = jnp.where(first >= 4, f0h[line], zero)
                low[to, :PW] = jnp.where(first >= 4, f0l[line], zero)
        between(1)
        for c in range(count):
            rows = []
            for g in range(lines):
                n = i * G + c * lines + g
                line = slice(g * T, g * T + T)
                row = []
                for j in range(4):
                    keep = jnp.logical_and(tab[F_PAT + n * 8 + 4 + j] != 0, tab[F_AT + n] >= 4)
                    part = ups[c][line, j * T : j * T + T]
                    old = rest[slot, c * SUB + g * T : c * SUB + g * T + T, j * T : j * T + T]
                    row.append(old - jnp.where(keep, part, 0.0))
                rows.append(jnp.concatenate(row, axis=1))
            f1.append(by_inverse(*halves(jnp.concatenate(rows, axis=0)), i2h, i2l))
        between(2)
        for c in range(count):
            f1h, f1l = halves(f1[c])
            for g in range(lines):
                first = tab[F_AT + i * G + c * lines + g]
                line, to = slice(g * T, g * T + T), slice(c * SUB + g * T, c * SUB + g * T + T)
                high[to, PW:] = jnp.where(first >= 8, f1h[line], zero)
                low[to, PW:] = jnp.where(first >= 8, f1l[line], zero)
        return list(zip(f0, f1))

    @pl.when(step == 0)
    def _():
        load(0).start()
        load(1).start()
        tiles[16, 0] = jnp.zeros((64, T), BF16)
        load(0).wait()
        load(1).wait()
        for g in range(G):
            assemble(step, 0, g)

    @pl.when(step > 0)
    def _():
        slot = step % 2
        nxt = jnp.minimum(step, STEPS - 1)

        def between(k):
            for g in range(G):
                if g * 3 // G == k:
                    assemble(nxt, slot, g)

        keep = multiply(step - 1, 1 - slot, between)
        for g in range(G):
            c, e = divmod(g, SUB // T)

            @pl.when(tab[F_SHARE] == (step - 1) * G + g)
            def _():
                f0, f1 = keep[c]
                fac[:, :PW] = f0[e * T : e * T + T]
                fac[:, PW:] = jnp.where(tab[F_AT + (step - 1) * G + g] >= 4, f1[e * T : e * T + T], 0.0)


def factor_rows(tab, own_r, buf_q, buf_r, inverses):
    small = pl.BlockSpec((PW, PW), lambda i, tab: (0, 0), pipeline_mode=pl.Buffered(1))
    out = pl.BlockSpec((TM, 1024), lambda i, tab: (jnp.maximum(i - 1, 0), 0))
    shape = jax.ShapeDtypeStruct((3072, 1024), BF16)
    return pl.pallas_call(
        factor_kernel,
        out_shape=(shape, shape, jax.ShapeDtypeStruct((T, 1024), F32)),
        grid_spec=pltpu.PrefetchScalarGridSpec(
            num_scalar_prefetch=1,
            grid=(STEPS + 1,),
            in_specs=[
                pl.BlockSpec((G, 16, 64, T), lambda i, tab: (jnp.minimum(i, QS - 1), 2, 0, 0)),
                pl.BlockSpec((TM, 1024), lambda i, tab: (jnp.clip(i - QS, 0, RS - 1), 0)),
                pl.BlockSpec(memory_space=pl.ANY),
                pl.BlockSpec(memory_space=pl.ANY),
            ]
            + [small] * 6,
            out_specs=[out, out, pl.BlockSpec((T, 1024), lambda i, tab: (0, 0))],
            scratch_shapes=[
                pltpu.VMEM((2, TM, PW), BF16),
                pltpu.VMEM((2, TM, PW), BF16),
                pltpu.VMEM((2, TM, PW), F32),
                pltpu.VMEM((17, 32, 64, T), BF16),
                pltpu.SemaphoreType.DMA((2,)),
            ],
        ),
        compiler_params=pltpu.CompilerParams(vmem_limit_bytes=VMEM),
        cost_estimate=pl.CostEstimate(
            flops=16 * 10**9, bytes_accessed=30 * MIB, transcendentals=0
        ),
        name="factor_rows",
    )(tab, buf_q, own_r, buf_q, buf_r.reshape(8, 32, 64, T), *inverses)


UM = 256
UG = UM // T
U_ROW, U_COL, U_PAT, U_LEFT = 0, 32, 48, 176


def update_kernel(tab, qh, ql, rh, rl, own, *rest):
    bufs, out = rest[: 2 * UG], rest[2 * UG]
    n = pl.program_id(0) * UG
    at_left = tab[U_LEFT] == 0
    fh, fl = rh[...], rl[...]
    f3 = jnp.concatenate([fh, fh, fl], axis=1)
    for h in range(4):
        qr = slice(h * 256, h * 256 + 256)
        up = nt(f3, jnp.concatenate([qh[qr, :], ql[qr, :], qh[qr, :]], axis=1))
        for g in range(UG):
            for e in range(2):
                j = h * 2 + e
                at = slice(g * T, g * T + T), slice(j * T, j * T + T)
                x = jnp.where(at_left, own[at].astype(F32), 0.0)
                for c in range(2):
                    cs = tab[U_COL + c * 8 + j]
                    valid = jnp.logical_and(tab[U_ROW + c * 16 + n + g] >= 0, cs >= 0)
                    cs = jnp.maximum(cs, 0)
                    tile = jnp.concatenate(
                        [bufs[g * 2 + c][cs // 2, 0, i, 0, cs % 2] for i in range(2)], axis=0
                    )
                    x = x + jnp.where(valid, tile.astype(F32), 0.0)
                x = x - up[g * T : g * T + T, e * T : e * T + T]
                kept = tab[U_PAT + (n + g) * 8 + j] != 0
                out[at] = jnp.where(kept, x, 0.0).astype(BF16)


def update(tab, high, low, own, buf):
    once = pl.Buffered(1)
    block = pl.BlockSpec((UM, 1024), lambda i, tab: (i, 0))
    after = pl.BlockSpec((UM, 1024), lambda i, tab: (i + 1024 // UM, 0))

    def tiles(g, c):
        def at(i, tab):
            rs = jnp.maximum(tab[U_ROW + c * 16 + i * UG + g], 0)
            return 0, rs % 2, 0, c * 4 + rs // 2, 0, 0, 0

        return pl.BlockSpec((4, 1, 2, 1, 2, 64, T), at)

    whole = pl.BlockSpec((1024, 1024), lambda i, tab: (0, 0), pipeline_mode=once)
    return pl.pallas_call(
        update_kernel,
        out_shape=jax.ShapeDtypeStruct((2048, 1024), BF16),
        grid_spec=pltpu.PrefetchScalarGridSpec(
            num_scalar_prefetch=1,
            grid=(2048 // UM,),
            in_specs=[whole, whole, after, after, block]
            + [tiles(g, c) for g in range(UG) for c in range(2)],
            out_specs=block,
        ),
        compiler_params=pltpu.CompilerParams(vmem_limit_bytes=VMEM),
        cost_estimate=pl.CostEstimate(
            flops=13 * 10**9, bytes_accessed=36 * MIB, transcendentals=0
        ),
        name="update",
    )(tab, high, low, high, low, own, *([buf] * (2 * UG)))


def shift(x, axis, k):
    return lax.ppermute(x, axis, [(i, (i + k) % 4) for i in range(4)])


def swap(x):
    return lax.ppermute(x, "core", [(0, 1), (1, 0)])


def pick(x, n):
    return lax.dynamic_index_in_dim(x, n, 0, keepdims=False)


def select(n, *cases):
    return lax.select_n(n, *cases)


def body(children, child_maps, pattern, own_cols):
    z, core, y, x = (lax.axis_index(a) for a in ALL)
    row, col = z * 2 + core, y * 4 + x
    child = row // 4

    groups = child_maps.reshape(8, 16)
    home = groups // 16
    earlier = jnp.arange(16)[None, :] < jnp.arange(16)[:, None]
    rank = jnp.sum(((home[:, :, None] == home[:, None, :]) & earlier[None]).astype(I32), axis=2)
    slot = home * 2 + rank
    orders = jnp.sum(
        jnp.where(
            slot[:, None, :] == jnp.arange(16)[None, :, None], jnp.arange(16)[None, None, :], 0
        ),
        axis=2,
    )
    order = pick(orders, row)
    column_orders = pick(orders.reshape(2, 4, 16).transpose(1, 0, 2), y)
    columns = child_maps.reshape(2, 16, 4)
    mine_columns = pick(pick(columns, child), col)
    strip_at = jnp.sum(jnp.where(mine_columns < 8, jnp.arange(4), 0))

    mine = lax.dynamic_slice(children, (0, strip_at * T), (2048, T)).reshape(16, T, T)[order]
    from_x = column_orders[:, :2] // 4

    strip = lax.all_to_all(mine.reshape(32, 64, T), ROW + ("x",), 0, 0, tiled=True)
    packed = pack_rows(children, order.astype(I32))
    own_piece = lax.dynamic_slice(own_cols, (0, col * 64), (1024, 64))
    own_piece = own_piece.reshape(8, T, 64).transpose(1, 0, 2).reshape(T, 4, T)
    first = jnp.concatenate(
        [mine[:2].transpose(1, 0, 2), own_piece, jnp.zeros((T, 2, T), BF16)], axis=1
    )
    by_half = mine.reshape(4, 2, 2, T, T)
    along_x = [
        lax.dynamic_index_in_dim(by_half, (x + k) % 4 // 2, 1, keepdims=False) for k in range(4)
    ]
    halved = pick(own_cols.reshape(2, 4, 2, T, 1024), x % 2)
    kept = lax.dynamic_index_in_dim(halved, core, 1, keepdims=False)
    given = lax.dynamic_index_in_dim(halved, 1 - core, 1, keepdims=False)
    place = lambda z, c, y, x: ((z * 2 + c) * 4 + y) * 4 + x
    chips = [(y, x) for y in range(4) for x in range(4)]
    along_x, given, first, strip = lax.optimization_barrier((along_x, given, first, strip))
    strip = jnp.take_along_axis(
        strip.reshape(2, 4, 4, 64, T), from_x[:, None, :, None, None], axis=2
    )
    buf_r = lax.all_gather(strip, COL, axis=0, tiled=False).reshape(256, 64, T)
    first = lax.all_to_all(first, ALL, 0, 0, tiled=True)
    along_x = [along_x[0]] + [shift(along_x[k], "x", k) for k in range(1, 4)]
    given = lax.ppermute(
        given, ALL, [(place(b, a // 2, b, a), place(b, 1 - a // 2, b, a)) for b, a in chips]
    )
    steps = (x - pick(from_x, child)) % 4
    slots = jnp.stack([select(steps[s], *along_x) for s in range(2)])
    along_y = [
        lax.dynamic_index_in_dim(slots, (y + k) % 4, 1, keepdims=False) for k in range(4)
    ]
    along_y = [along_y[0]] + [shift(along_y[k], "y", k) for k in range(1, 4)]
    kept = jnp.where(core == x // 2, kept, given)
    along_z = [pick(kept, (z + k) % 4) for k in range(4)]
    for k in range(1, 4):
        along_z[k] = lax.ppermute(
            along_z[k],
            ALL,
            [(place(b, c, b, a), place((b + k) % 4, c, b, a)) for b, a in chips for c in range(2)],
        )

    lead_row = jnp.sum(
        jnp.where(slot[:, None, :] == jnp.arange(2)[None, :, None], groups[:, None, :] + 1, 0), axis=2
    ) - 1
    lead_row = jnp.where(lead_row < 8, lead_row, -1)
    lead_col = jnp.sum(jnp.where(columns < 8, columns + 1, 0), axis=2) - 1
    lead_col = jnp.repeat(lead_col, 4, axis=0)
    tile = jnp.where(
        (lead_row[:, None, :] >= 0) & (lead_col[:, :, None] >= 0),
        lead_row[:, None, :] * 8 + lead_col[:, :, None],
        -1,
    ).reshape(256)
    wanted = jnp.array([i * 8 + j for i, j in LOWER])
    spread = (tile[None, :] == wanted[:, None]).astype(BF16)
    lead = nn(spread, first[:, :2].reshape(256, T))
    lead_own = first[:16, 2:6].reshape(16, 8, 64).transpose(1, 0, 2).reshape(64, T)
    lead_own = jnp.concatenate([lead_own[8 * i : 8 * i + i + 1] for i in range(8)], axis=0)
    lead = jnp.broadcast_to((lead + lead_own.astype(F32))[None], (16, 36, T))

    lead = lax.all_to_all(lead, COL, 0, 0, tiled=True)
    by_shift = [lead] + [shift(lead, "z", k) for k in range(1, 4)]
    by_shift, along_y, along_z, packed = lax.optimization_barrier(
        (by_shift, along_y, along_z, packed)
    )
    here = lax.all_to_all(packed, ROW + ("x",), 0, 0, tiled=True).reshape(128, 64, T)
    own_q = jnp.where(z == y, along_z[0], 0) + along_z[1] + along_z[2] + along_z[3]
    own_q = own_q.reshape(2, 64, 8, T).transpose(2, 0, 1, 3).reshape(16, 64, T)
    parts = jnp.concatenate([jnp.stack(along_y).reshape(32, 64, T), own_q], axis=0)
    buf_q = lax.all_gather(parts, ROW, axis=0, tiled=False)
    lead = jnp.stack([select((z - n) % 4, *by_shift) for n in range(4)])
    other = swap(lead)
    lead = jnp.where(
        core == 0, jnp.stack([lead, other], axis=1), jnp.stack([other, lead], axis=1)
    ).reshape(128, 36, T).transpose(1, 0, 2)

    i1, i1h, i1l = panel_call(
        panel1_kernel, "panel1", 10, (F32, BF16, BF16), [(PW, PW), (T, T)], lead
    )
    i1, here = lax.optimization_barrier((i1, here))
    packed = pack_columns(here, column_orders.astype(I32).reshape(-1))
    tiles = lax.all_to_all(packed, COL, 0, 0, tiled=True).reshape(4, 2, 2, 8, 2, 64, T)
    i1, packed = lax.optimization_barrier((i1, packed))
    lh, ll, i2h, i2l = panel_call(
        panel2_kernel,
        "panel2",
        36,
        (BF16,) * 4,
        [(PW, PW), (PW, PW), (T, T), (PW, PW)],
        lead,
        i1,
    )

    by_child = groups.reshape(2, 64)
    ranks = rank.reshape(2, 4, 16)
    group = jnp.arange(4)[None, :, None]

    def find(first, count, values):
        hit = by_child[:, None, :] == (first + jnp.arange(count))[None, :, None]
        return jnp.sum(jnp.where(hit, values.reshape(2, 1, 64) + 1, 0), axis=2) - 1

    row_source = find(row * 16, 16, group * 2 + ranks).reshape(-1)
    col_source = find(col * 8, 8, group * 2 + ranks).reshape(-1)
    row_group = jnp.arange(8).reshape(2, 4, 1)
    q_rows = find(col * 8, 8, row_group * 32 + ranks * 2)
    r_rows = find(row * 16, 16, ranks * 32 + row_group * 2)
    q_cols = find(0, 8, (y - group) % 4 * 8 + ranks * 4)
    r_cols = find(0, 8, group * 64 + ranks)
    pat_rows = lax.dynamic_slice(pattern, (row * 16, 0), (16, 128))
    factor_tab = jnp.concatenate(
        [
            q_rows.T.reshape(-1),
            r_rows.T.reshape(-1),
            q_cols.reshape(-1),
            r_cols.reshape(-1),
            lax.dynamic_slice(pattern, (col * 8, 0), (8, 8)).reshape(-1),
            pat_rows[:, :8].reshape(-1),
            col * 8 + jnp.arange(8),
            row * 16 + jnp.arange(16),
            jnp.stack([8 + col]),
        ]
    ).astype(I32)
    update_tab = jnp.concatenate(
        [
            row_source,
            col_source,
            lax.dynamic_slice(pat_rows, (0, col * 8), (16, 8)).reshape(-1),
            jnp.stack([col]),
        ]
    ).astype(I32)
    high, low, fac = factor_rows(
        factor_tab, own_cols, buf_q, buf_r, (i1h, i1l, lh, ll, i2h, i2l)
    )
    return update(update_tab, high, low, own_cols, tiles), fac


def solution(mesh):
    grid = Mesh(mesh.devices.reshape(4, 2, 4, 4), ALL)
    return jax.shard_map(
        body,
        mesh=grid,
        in_specs=(P(ROW, COL), P(), P(), P(ROW, None)),
        out_specs=(P(ROW, COL), P(ALL, None)),
        check_vma=False,
    )
```

profile of v0, /device:TPU:0, one launch (start us, length us, event | category | flops | bytes accessed | tf_op | source)
XLA Modules:
  0.0 253.3 jit_solution(6080518421361270699)
XLA Ops:
  13.1 8.2 %all-to-all-start = ((bf16[32,64,128]{2,1,0:T(8,128)(2,1)}), bf16[32,64,128]{2,1,0:T(8,128)(2,1)S(1)}, u32[]{:S(2)}, u32[]{:S(2)}) async-start(bf16[32,64,128]{2,1,0:T(8,128)(2,1)} %bitcast.21), calls=%async_computation | async-start | bytes 1048576 | tf_op jit(solution)/shard_map/all_to_all | solution.py:483
  25.2 2.3 dynamic-slice_bitcast_fusion
  27.4 2.0 dynamic-slice_bitcast_fusion.5
  29.6 3.5 %all-to-all-done = bf16[32,64,128]{2,1,0:T(8,128)(2,1)S(1)} async-done(((bf16[32,64,128]{2,1,0:T(8,128)(2,1)}), bf16[32,64,128]{2,1,0:T(8,128)(2,1)S(1)}, u32[]{:S(2)}, u32[]{:S(2)}) %all-to-all-start) | async-done | bytes 524320 | tf_op jit(solution)/shard_map/all_to_all | solution.py:483
  35.7 6.9 %all-to-all-start.1 = ((bf16[128,8,128]{2,1,0:T(8,128)(2,1)}), bf16[128,8,128]{2,1,0:T(8,128)(2,1)S(1)}, u32[]{:S(2)}, u32[]{:S(2)}) async-start(bf16[128,8,128]{2,1,0:T(8,128)(2,1)} %copy.69), calls=%async_computation.1 | async-start | bytes 524288 | tf_op jit(solution)/shard_map/all_to_all | solution.py:504
  56.9 3.5 %all-to-all-start.2 = ((f32[16,36,128]{2,1,0:T(8,128)}), f32[16,36,128]{2,1,0:T(8,128)S(1)}, u32[]{:S(2)}, u32[]{:S(2)}) async-start(f32[16,36,128]{2,1,0:T(8,128)} %broadcast_in_dim.146), calls=%async_computation.2 | async-start | bytes 655360 | tf_op jit(solution)/shard_map/all_to_all | solution.py:542
  60.6 6.1 %collective-permute-done.4 = bf16[4,2,128,128]{3,2,1,0:T(8,128)(2,1)S(1)} collective-permute-done((bf16[4,2,128,128]{3,2,1,0:T(8,128)(2,1)S(1)}, bf16[4,2,128,128]{3,2,1,0:T(8,128)(2,1)S(1)}, u32[]{:S(2)}, u32[]{:S(2)}) %collective-permute-start.4) | collective-permute-done | bytes 262176 | tf_op jit(solution)/shard_map/ppermute | solution.py:443
  68.6 2.0 collective-permute-start.8
  70.6 2.2 collective-permute-start.7
  72.8 3.3 %collective-permute-start.2 = (f32[16,36,128]{2,1,0:T(8,128)S(1)}, f32[16,36,128]{2,1,0:T(8,128)S(1)}, u32[]{:S(2)}, u32[]{:S(2)}) collective-permute-start(f32[16,36,128]{2,1,0:T(8,128)S(1)} %all-to-all-done.2), channel_id=1, source_target_pairs={{0,96},{32,0},{64,32},{96,64},{1,97},{33,1},{65,33},{97,65},{2,98}... | collective-permute-start | bytes 884744 | tf_op jit(solution)/shard_map/ppermute | solution.py:443
  82.3 7.3 %collective-permute-start.12 = (bf16[128,1024]{1,0:T(8,128)(2,1)}, bf16[128,1024]{1,0:T(8,128)(2,1)}, u32[]{:S(2)}, u32[]{:S(2)}) collective-permute-start(bf16[128,1024]{1,0:T(8,128)(2,1)} %get-tuple-element.86), channel_id=1, source_target_pairs={{0,96},{16,112},{1,97},{17,113},{2,98},{18,114},{3,99},{19,115},{3... | collective-permute-start | bytes 786440 | tf_op jit(solution)/shard_map/ppermute | solution.py:518
  89.5 2.2 collective-permute-start.11
  92.5 2.0 collective-permute-start.10
  94.5 3.6 %pack_rows.1 = bf16[32,4,64,128]{3,2,1,0:T(8,128)(2,1)} custom-call(s32[16]{0:T(128)S(1)} %fusion.26.tab, bf16[2048,512]{1,0:T(8,128)(2,1)S(1)} %copy-done.1, bf16[2048,512]{1,0:T(8,128)(2,1)S(1)} %copy-done.1), custom_call_target="tpu_custom_call" | custom-call | bytes 4194304 | tf_op jit(solution)/shard_map/pack_rows/pallas_call | solution.py:181
  98.1 3.1 %collective-permute-done.10 = bf16[128,1024]{1,0:T(8,128)(2,1)} collective-permute-done((bf16[128,1024]{1,0:T(8,128)(2,1)S(1)}, bf16[128,1024]{1,0:T(8,128)(2,1)}, u32[]{:S(2)}, u32[]{:S(2)}) %collective-permute-start.10) | collective-permute-done | bytes 262176 | tf_op jit(solution)/shard_map/ppermute | solution.py:518
  112.0 6.8 %all-to-all-start.3 = ((bf16[32,4,64,128]{3,2,1,0:T(8,128)(2,1)}), bf16[32,4,64,128]{3,2,1,0:T(8,128)(2,1)S(1)}, u32[]{:S(2)}, u32[]{:S(2)}) async-start(bf16[32,4,64,128]{3,2,1,0:T(8,128)(2,1)} %pack_rows.1), calls=%async_computation.3 | async-start | bytes 4194304 | tf_op jit(solution)/shard_map/all_to_all | solution.py:547
  121.1 22.9 %panel1.1 = (f32[512,512]{1,0:T(8,128)S(1)}, bf16[512,512]{1,0:T(8,128)(2,1)S(1)}, bf16[512,512]{1,0:T(8,128)(2,1)S(1)}) custom-call(f32[36,128,128]{2,1,0:T(8,128)S(1)} %bitcast.120), custom_call_target="tpu_custom_call" | custom-call | flops 24999999488 | bytes 4194304 | tf_op jit(solution)/shard_map/panel1/pallas_call | solution.py:159
  147.0 4.4 %all-to-all-done.3 = bf16[32,4,64,128]{3,2,1,0:T(8,128)(2,1)S(1)} async-done(((bf16[32,4,64,128]{3,2,1,0:T(8,128)(2,1)}), bf16[32,4,64,128]{3,2,1,0:T(8,128)(2,1)S(1)}, u32[]{:S(2)}, u32[]{:S(2)}) %all-to-all-start.3) | async-done | bytes 2097184 | tf_op jit(solution)/shard_map/all_to_all | solution.py:547
  152.7 2.0 copy-done
  154.7 7.4 %all-to-all-start.4 = ((bf16[16,8,2,64,128]{4,3,2,1,0:T(8,128)(2,1)}), bf16[16,8,2,64,128]{4,3,2,1,0:T(8,128)(2,1)}, u32[]{:S(2)}, u32[]{:S(2)}) async-start(bf16[16,8,2,64,128]{4,3,2,1,0:T(8,128)(2,1)} %copy-done), calls=%async_computation.4 | async-start | bytes 8388608 | tf_op jit(solution)/shard_map/all_to_all | solution.py:563
  162.7 26.8 %panel2.1 = (bf16[512,512]{1,0:T(8,128)(2,1)S(1)}, bf16[512,512]{1,0:T(8,128)(2,1)S(1)}, bf16[512,512]{1,0:T(8,128)(2,1)S(1)}, bf16[512,512]{1,0:T(8,128)(2,1)S(1)}) custom-call(f32[36,128,128]{2,1,0:T(8,128)S(1)} %bitcast.121, f32[512,512]{1,0:T(8,128)S(1)} %get-tuple-element.60.i1_ref), custom_call_target="tpu_custom_call" | custom-call | flops 24999999488 | bytes 4194304 | tf_op jit(solution)/shard_map/panel2/pallas_call | solution.py:159
  192.7 27.7 %factor_rows.1 = (bf16[3072,1024]{1,0:T(8,128)(2,1)}, bf16[3072,1024]{1,0:T(8,128)(2,1)}, f32[128,1024]{1,0:T(8,128)}) custom-call(s32[297]{0:T(512)} %concatenate.16.tab, bf16[8,48,64,128]{3,2,1,0:T(8,128)(2,1)} %bitcast.141, bf16[2048,1024]{1,0:T(8,128)(2,1)} %own.1, bf16[8,48,64,128]{3,2,1,0:T(8,128)(2,1)} %bitcast.142, ...), custom_call_target="tpu_custom_call" | custom-call | flops 16000000000 | bytes 31457280 | tf_op jit(solution)/shard_map/factor_rows/pallas_call | solution.py:349
  220.4 4.1 %all-to-all-done.4 = bf16[16,8,2,64,128]{4,3,2,1,0:T(8,128)(2,1)} async-done(((bf16[16,8,2,64,128]{4,3,2,1,0:T(8,128)(2,1)}), bf16[16,8,2,64,128]{4,3,2,1,0:T(8,128)(2,1)}, u32[]{:S(2)}, u32[]{:S(2)}) %all-to-all-start.4) | async-done | bytes 4194336 | tf_op jit(solution)/shard_map/all_to_all | solution.py:563
  224.5 21.9 %update.1 = bf16[2048,1024]{1,0:T(8,128)(2,1)} custom-call(s32[177]{0:T(256)} %pad_add_fusion.tab, bf16[3072,1024]{1,0:T(8,128)(2,1)} %get-tuple-element.65.qh.rh, bf16[3072,1024]{1,0:T(8,128)(2,1)} %get-tuple-element.66.ql.rl, bf16[3072,1024]{1,0:T(8,128)(2,1)} %get-tuple-element.65.qh.rh, bf16[3072,1024]{1,0:T(8,128)(2,1)} %get-tuple-element.66.ql.rl, ...), custom_call_target="tpu_custom_call" | custom-call | flops 12999999488 | bytes 37748736 | tf_op jit(solution)/shard_map/update/pallas_call | solution.py:424
  (175 shorter events, 51.8 us)
Async XLA Ops:
  13.1 20.0 %all-to-all-start = ((bf16[32,64,128]{2,1,0:T(8,128)(2,1)}), bf16[32,64,128]{2,1,0:T(8,128)(2,1)S(1)}, u32[]{:S(2)}, u32[]{:S(2)}) async-start(bf16[32,64,128]{2,1,0:T(8,128)(2,1)} %bitcast.21), calls=%async_computation | async-start | bytes 1048576 | tf_op jit(solution)/shard_map/all_to_all | solution.py:483
  21.3 171.4 %all-gather.4.cloned.1.call-start = ((), (), s32[]{:S(2)}) async-start(), calls=%async_computation.5 | async-start | bytes 4456448 | tf_op jit(solution)/shard_map/all_gather | solution.py:503
  29.5 26.5 %copy-start.14 = (s32[36]{0:T(128)S(1)}, s32[36]{0:T(128)}, u32[]{:S(2)}) copy-start(s32[36]{0:T(128)} %constant.399.clone) | copy-start | bytes 436
  35.7 19.4 %all-to-all-start.1 = ((bf16[128,8,128]{2,1,0:T(8,128)(2,1)}), bf16[128,8,128]{2,1,0:T(8,128)(2,1)S(1)}, u32[]{:S(2)}, u32[]{:S(2)}) async-start(bf16[128,8,128]{2,1,0:T(8,128)(2,1)} %copy.69), calls=%async_computation.1 | async-start | bytes 524288 | tf_op jit(solution)/shard_map/all_to_all | solution.py:504
  42.7 33.4 %collective-permute-start.9 = (bf16[4,128,1024]{2,1,0:T(8,128)(2,1)}, bf16[4,128,1024]{2,1,0:T(8,128)(2,1)S(1)}, u32[]{:S(2)}, u32[]{:S(2)}) collective-permute-start(bf16[4,128,1024]{2,1,0:T(8,128)(2,1)} %dynamic-slice_bitcast_fusion), channel_id=1, source_target_pairs={{0,16},{1,17},{18,2},{19,3},{36,52},{37,53},{54,38},{55,39},{72,88... | collective-permute-start | bytes 3145736 | tf_op jit(solution)/shard_map/ppermute | solution.py:506
  48.9 11.6 %collective-permute-start.3 = (bf16[4,2,128,128]{3,2,1,0:T(8,128)(2,1)}, bf16[4,2,128,128]{3,2,1,0:T(8,128)(2,1)S(1)}, u32[]{:S(2)}, u32[]{:S(2)}) collective-permute-start(bf16[4,2,128,128]{3,2,1,0:T(8,128)(2,1)} %get-tuple-element.37), channel_id=1, source_target_pairs={{0,1},{1,2},{2,3},{3,0},{4,5},{5,6},{6,7},{7,4},{8,9},{9,10},{10,1... | collective-permute-start | bytes 786440 | tf_op jit(solution)/shard_map/ppermute | solution.py:443
  50.7 16.0 %collective-permute-start.4 = (bf16[4,2,128,128]{3,2,1,0:T(8,128)(2,1)S(1)}, bf16[4,2,128,128]{3,2,1,0:T(8,128)(2,1)S(1)}, u32[]{:S(2)}, u32[]{:S(2)}) collective-permute-start(bf16[4,2,128,128]{3,2,1,0:T(8,128)(2,1)S(1)} %get-tuple-element.38), channel_id=1, source_target_pairs={{0,2},{1,3},{2,0},{3,1},{4,6},{5,7},{6,4},{7,5},{8,10},{9,11},{10,... | collective-permute-start | bytes 786440 | tf_op jit(solution)/shard_map/ppermute | solution.py:443
  52.5 14.2 %collective-permute-start.5 = (bf16[4,2,128,128]{3,2,1,0:T(8,128)(2,1)S(1)}, bf16[4,2,128,128]{3,2,1,0:T(8,128)(2,1)}, u32[]{:S(2)}, u32[]{:S(2)}) collective-permute-start(bf16[4,2,128,128]{3,2,1,0:T(8,128)(2,1)S(1)} %get-tuple-element.39), channel_id=1, source_target_pairs={{0,3},{1,0},{2,1},{3,2},{4,7},{5,4},{6,5},{7,6},{8,11},{9,8},{10,9... | collective-permute-start | bytes 786440 | tf_op jit(solution)/shard_map/ppermute | solution.py:443
  56.9 15.9 %all-to-all-start.2 = ((f32[16,36,128]{2,1,0:T(8,128)}), f32[16,36,128]{2,1,0:T(8,128)S(1)}, u32[]{:S(2)}, u32[]{:S(2)}) async-start(f32[16,36,128]{2,1,0:T(8,128)} %broadcast_in_dim.146), calls=%async_computation.2 | async-start | bytes 655360 | tf_op jit(solution)/shard_map/all_to_all | solution.py:542
  60.5 132.2 %all-gather.6.cloned.1.call-start = ((), (), s32[]{:S(2)}) async-start(), calls=%async_computation.6 | async-start | bytes 7077888 | tf_op jit(solution)/shard_map/all_gather | solution.py:551
  68.6 9.7 %collective-permute-start.8 = (bf16[2,2,128,128]{3,2,1,0:T(8,128)(2,1)}, bf16[2,2,128,128]{3,2,1,0:T(8,128)(2,1)}, u32[]{:S(2)}, u32[]{:S(2)}) collective-permute-start(bf16[2,2,128,128]{3,2,1,0:T(8,128)(2,1)} %get-tuple-element.92), channel_id=1, source_target_pairs={{0,12},{4,0},{8,4},{12,8},{1,13},{5,1},{9,5},{13,9},{2,14},{6,2},{... | collective-permute-start | bytes 393224 | tf_op jit(solution)/shard_map/ppermute | solution.py:443
  70.6 11.7 %collective-permute-start.6 = (bf16[2,2,128,128]{3,2,1,0:T(8,128)(2,1)}, bf16[2,2,128,128]{3,2,1,0:T(8,128)(2,1)}, u32[]{:S(2)}, u32[]{:S(2)}) collective-permute-start(bf16[2,2,128,128]{3,2,1,0:T(8,128)(2,1)} %get-tuple-element.94), channel_id=1, source_target_pairs={{0,4},{4,8},{8,12},{12,0},{1,5},{5,9},{9,13},{13,1},{2,6},{6,10},{... | collective-permute-start | bytes 393224 | tf_op jit(solution)/shard_map/ppermute | solution.py:443
  70.6 23.8 %copy-start.1 = (bf16[2048,512]{1,0:T(8,128)(2,1)S(1)}, bf16[2048,512]{1,0:T(8,128)(2,1)}, u32[]{:S(2)}) copy-start(bf16[2048,512]{1,0:T(8,128)(2,1)} %low.1) | copy-start | bytes 6291460
  70.6 18.9 %collective-permute-start.7 = (bf16[2,2,128,128]{3,2,1,0:T(8,128)(2,1)}, bf16[2,2,128,128]{3,2,1,0:T(8,128)(2,1)}, u32[]{:S(2)}, u32[]{:S(2)}) collective-permute-start(bf16[2,2,128,128]{3,2,1,0:T(8,128)(2,1)} %get-tuple-element.95), channel_id=1, source_target_pairs={{0,8},{4,12},{8,0},{12,4},{1,9},{5,13},{9,1},{13,5},{2,10},{6,14},... | collective-permute-start | bytes 393224 | tf_op jit(solution)/shard_map/ppermute | solution.py:443
  72.8 18.9 %collective-permute-start.2 = (f32[16,36,128]{2,1,0:T(8,128)S(1)}, f32[16,36,128]{2,1,0:T(8,128)S(1)}, u32[]{:S(2)}, u32[]{:S(2)}) collective-permute-start(f32[16,36,128]{2,1,0:T(8,128)S(1)} %all-to-all-done.2), channel_id=1, source_target_pairs={{0,96},{32,0},{64,32},{96,64},{1,97},{33,1},{65,33},{97,65},{2,98}... | collective-permute-start | bytes 884744 | tf_op jit(solution)/shard_map/ppermute | solution.py:443
  76.1 22.0 %collective-permute-start.1 = (f32[16,36,128]{2,1,0:T(8,128)S(1)}, f32[16,36,128]{2,1,0:T(8,128)}, u32[]{:S(2)}, u32[]{:S(2)}) collective-permute-start(f32[16,36,128]{2,1,0:T(8,128)S(1)} %all-to-all-done.2), channel_id=1, source_target_pairs={{0,64},{32,96},{64,0},{96,32},{1,65},{33,97},{65,1},{97,33},{2,66}... | collective-permute-start | bytes 884744 | tf_op jit(solution)/shard_map/ppermute | solution.py:443
  78.3 19.8 %collective-permute-start = (f32[16,36,128]{2,1,0:T(8,128)S(1)}, f32[16,36,128]{2,1,0:T(8,128)S(1)}, u32[]{:S(2)}, u32[]{:S(2)}) collective-permute-start(f32[16,36,128]{2,1,0:T(8,128)S(1)} %all-to-all-done.2), channel_id=1, source_target_pairs={{0,32},{32,64},{64,96},{96,0},{1,33},{33,65},{65,97},{97,1},{2,34}... | collective-permute-start | bytes 884744 | tf_op jit(solution)/shard_map/ppermute | solution.py:443
  82.3 15.9 %collective-permute-start.12 = (bf16[128,1024]{1,0:T(8,128)(2,1)}, bf16[128,1024]{1,0:T(8,128)(2,1)}, u32[]{:S(2)}, u32[]{:S(2)}) collective-permute-start(bf16[128,1024]{1,0:T(8,128)(2,1)} %get-tuple-element.86), channel_id=1, source_target_pairs={{0,96},{16,112},{1,97},{17,113},{2,98},{18,114},{3,99},{19,115},{3... | collective-permute-start | bytes 786440 | tf_op jit(solution)/shard_map/ppermute | solution.py:518
  89.5 8.6 %collective-permute-start.11 = (bf16[128,1024]{1,0:T(8,128)(2,1)S(1)}, bf16[128,1024]{1,0:T(8,128)(2,1)}, u32[]{:S(2)}, u32[]{:S(2)}) collective-permute-start(bf16[128,1024]{1,0:T(8,128)(2,1)S(1)} %get-tuple-element.87), channel_id=1, source_target_pairs={{0,64},{16,80},{1,65},{17,81},{2,66},{18,82},{3,67},{19,83},{36,10... | collective-permute-start | bytes 786440 | tf_op jit(solution)/shard_map/ppermute | solution.py:518
  92.5 8.7 %collective-permute-start.10 = (bf16[128,1024]{1,0:T(8,128)(2,1)S(1)}, bf16[128,1024]{1,0:T(8,128)(2,1)}, u32[]{:S(2)}, u32[]{:S(2)}) collective-permute-start(bf16[128,1024]{1,0:T(8,128)(2,1)S(1)} %get-tuple-element.88), channel_id=1, source_target_pairs={{0,32},{16,48},{1,33},{17,49},{2,34},{18,50},{3,35},{19,51},{36,68... | collective-permute-start | bytes 786440 | tf_op jit(solution)/shard_map/ppermute | solution.py:518
  109.3 9.5 %collective-permute-start.13 = (f32[4,16,36,128]{3,1,2,0:T(8,128)}, f32[4,16,36,128]{3,1,2,0:T(8,128)}, u32[]{:S(2)}, u32[]{:S(2)}) collective-permute-start(f32[4,16,36,128]{3,1,2,0:T(8,128)} %copy.73), channel_id=1, source_target_pairs={{0,16},{16,0},{1,17},{17,1},{2,18},{18,2},{3,19},{19,3},{4,20},{20... | collective-permute-start | bytes 3538952 | tf_op jit(solution)/shard_map/ppermute | solution.py:447
  112.0 39.4 %all-to-all-start.3 = ((bf16[32,4,64,128]{3,2,1,0:T(8,128)(2,1)}), bf16[32,4,64,128]{3,2,1,0:T(8,128)(2,1)S(1)}, u32[]{:S(2)}, u32[]{:S(2)}) async-start(bf16[32,4,64,128]{3,2,1,0:T(8,128)(2,1)} %pack_rows.1), calls=%async_computation.3 | async-start | bytes 4194304 | tf_op jit(solution)/shard_map/all_to_all | solution.py:547
  154.7 8.0 %copy-start.3 = (f32[4,2,16,36,128]{4,2,1,0,3:T(8,128)S(1)}, f32[4,2,16,36,128]{4,2,1,0,3:T(8,128)}, u32[]{:S(2)}) copy-start(f32[4,2,16,36,128]{4,2,1,0,3:T(8,128)} %copy-done.2) | copy-start | bytes 7077892
  154.7 69.9 %all-to-all-start.4 = ((bf16[16,8,2,64,128]{4,3,2,1,0:T(8,128)(2,1)}), bf16[16,8,2,64,128]{4,3,2,1,0:T(8,128)(2,1)}, u32[]{:S(2)}, u32[]{:S(2)}) async-start(bf16[16,8,2,64,128]{4,3,2,1,0:T(8,128)(2,1)} %copy-done), calls=%async_computation.4 | async-start | bytes 8388608 | tf_op jit(solution)/shard_map/all_to_all | solution.py:563
  (12 other events, 22.0 us)
Sparse Core Ops, SparseCore 0:
  34.6 60.7 all-gather.3
  104.8 64.3 all-gather.5
where the time goes:
time: 254 us; the launch traced here: 253 us
  Pallas kernels  104 us (41%)
  starting transfers between devices  60.6 us (24%)
  local copies, waits for them, and re-layouts  33.9 us (13%)
  waiting for transfers between devices  24.2 us (10%)
  between operations  19.3 us (8%)
  other arithmetic  10.8 us (4%)
    pallas_call x2, Pallas kernels, panel_call(): pl.pallas_call(kernel, out_shape=tuple((jax.ShapeDtypeStruct((PW, PW), t)...  49.7 us
    pallas_call x1, Pallas kernels, factor_rows(): pl.pallas_call(factor_kernel, out_shape=(shape, shape, jax.ShapeDtypeStru...  27.7 us
    pallas_call x1, Pallas kernels, update(): pl.pallas_call(update_kernel, out_shape=jax.ShapeDtypeStruct((2048, 1024)...  21.9 us
    ppermute x9, starting transfers between devices, shift(): return lax.ppermute(x, axis, [(i, (i + k) % 4) for i in range(4)])  14.8 us
    ppermute x3, starting transfers between devices, body(): lax.ppermute(along_z[k], ALL, [(place(b, c, b, a), place((b + k) % 4, c,...  11.5 us
    unnamed x31, local copies, waits for them, and re-layouts  9.09 us
    all_to_all x1, starting transfers between devices, body(): lax.all_to_all(mine.reshape(32, 64, T), ROW + ('x',), 0, 0, tiled=True)  8.24 us
    ppermute x9, waiting for transfers between devices, shift(): return lax.ppermute(x, axis, [(i, (i + k) % 4) for i in range(4)])  7.94 us
  transfers between devices with their start and end apart: 21, of which 7 were waited for; matrix products, arithmetic and copies ran while one was open for 12% of the time, Pallas kernels for 32%

commit v1 on v0

--- a/solution.py
+++ b/solution.py
@@ -50,8 +50,7 @@
 
 
 def rsqrt(d):
-    r = lax.rsqrt(d)
-    return r * (1.5 - 0.5 * d * r * r)
+    return lax.rsqrt(d)
 
 
 def invert_block(load, store):
@@ -164,7 +163,7 @@
         + [whole] * len(args),
         out_specs=[whole] * len(outs),
         scratch_shapes=[pltpu.VMEM(x, F32) for x in scratch],
-        compiler_params=pltpu.CompilerParams(vmem_limit_bytes=24 * MIB),
+        compiler_params=pltpu.CompilerParams(vmem_limit_bytes=VMEM),
         cost_estimate=pl.CostEstimate(flops=25 * 10**9, bytes_accessed=4 * MIB, transcendentals=0),
         name=name,
     )(lead, *args)

time: 254 us -> 254 us (level)
  waiting for transfers between devices: 24.2 us -> 29.6 us
  local copies, waits for them, and re-layouts: 33.9 us -> 29 us
    unnamed x31 -> x15, local copies, waits for them, and re-layouts: 9.09 us -> 2.8 us
    all_to_all x1, waiting for transfers between devices: 4.13 us -> 7.13 us  [body(): lax.all_to_all(packed, COL, 0, 0, tiled=True).reshape(4, 2, 2, 8, 2, 64, T)]
where the time goes in v1:
time: 254 us; the launch traced here: 253 us
  Pallas kernels  104 us (41%)
  starting transfers between devices  60.4 us (24%)
  waiting for transfers between devices  29.6 us (12%)
  local copies, waits for them, and re-layouts  29 us (11%)
  between operations  19.4 us (8%)
  other arithmetic  10.9 us (4%)
    pallas_call x2, Pallas kernels, panel_call(): pl.pallas_call(kernel, out_shape=tuple((jax.ShapeDtypeStruct((PW, PW), t)...  49.1 us
    pallas_call x1, Pallas kernels, factor_rows(): pl.pallas_call(factor_kernel, out_shape=(shape, shape, jax.ShapeDtypeStru...  27.7 us
    pallas_call x1, Pallas kernels, update(): pl.pallas_call(update_kernel, out_shape=jax.ShapeDtypeStruct((2048, 1024)...  21.9 us
    ppermute x9, starting transfers between devices, shift(): return lax.ppermute(x, axis, [(i, (i + k) % 4) for i in range(4)])  14.8 us
    ppermute x3, starting transfers between devices, body(): lax.ppermute(along_z[k], ALL, [(place(b, c, b, a), place((b + k) % 4, c,...  11.4 us
    all_to_all x1, starting transfers between devices, body(): lax.all_to_all(mine.reshape(32, 64, T), ROW + ('x',), 0, 0, tiled=True)  8.24 us
    ppermute x9, waiting for transfers between devices, shift(): return lax.ppermute(x, axis, [(i, (i + k) % 4) for i in range(4)])  8 us
    all_to_all x1, starting transfers between devices, body(): lax.all_to_all(packed, COL, 0, 0, tiled=True).reshape(4, 2, 2, 8, 2, 64, T)  7.14 us
  transfers between devices with their start and end apart: 21, of which 7 were waited for; matrix products, arithmetic and copies ran while one was open for 12% of the time, Pallas kernels for 32%

profile of v1, /device:TPU:0, one launch (start us, length us, event | category | flops | bytes accessed | tf_op | source)
XLA Modules:
  0.0 253.1 jit_solution(5790863134908891678)
XLA Ops:
  13.1 8.2 %all-to-all-start = ((bf16[32,64,128]{2,1,0:T(8,128)(2,1)}), bf16[32,64,128]{2,1,0:T(8,128)(2,1)S(1)}, u32[]{:S(2)}, u32[]{:S(2)}) async-start(bf16[32,64,128]{2,1,0:T(8,128)(2,1)} %bitcast.21), calls=%async_computation | async-start | bytes 1048576 | tf_op jit(solution)/shard_map/all_to_all | solution.py:482
  25.2 2.3 dynamic-slice_bitcast_fusion
  27.4 2.1 dynamic-slice_bitcast_fusion.5
  29.6 3.5 %all-to-all-done = bf16[32,64,128]{2,1,0:T(8,128)(2,1)S(1)} async-done(((bf16[32,64,128]{2,1,0:T(8,128)(2,1)}), bf16[32,64,128]{2,1,0:T(8,128)(2,1)S(1)}, u32[]{:S(2)}, u32[]{:S(2)}) %all-to-all-start) | async-done | bytes 524320 | tf_op jit(solution)/shard_map/all_to_all | solution.py:482
  35.8 6.9 %all-to-all-start.1 = ((bf16[128,8,128]{2,1,0:T(8,128)(2,1)}), bf16[128,8,128]{2,1,0:T(8,128)(2,1)S(1)}, u32[]{:S(2)}, u32[]{:S(2)}) async-start(bf16[128,8,128]{2,1,0:T(8,128)(2,1)} %copy.69), calls=%async_computation.1 | async-start | bytes 524288 | tf_op jit(solution)/shard_map/all_to_all | solution.py:503
  57.0 3.5 %all-to-all-start.2 = ((f32[16,36,128]{2,1,0:T(8,128)}), f32[16,36,128]{2,1,0:T(8,128)S(1)}, u32[]{:S(2)}, u32[]{:S(2)}) async-start(f32[16,36,128]{2,1,0:T(8,128)} %broadcast_in_dim.146), calls=%async_computation.2 | async-start | bytes 655360 | tf_op jit(solution)/shard_map/all_to_all | solution.py:541
  60.6 6.2 %collective-permute-done.4 = bf16[4,2,128,128]{3,2,1,0:T(8,128)(2,1)S(1)} collective-permute-done((bf16[4,2,128,128]{3,2,1,0:T(8,128)(2,1)S(1)}, bf16[4,2,128,128]{3,2,1,0:T(8,128)(2,1)S(1)}, u32[]{:S(2)}, u32[]{:S(2)}) %collective-permute-start.4) | collective-permute-done | bytes 262176 | tf_op jit(solution)/shard_map/ppermute | solution.py:442
  68.6 2.0 collective-permute-start.8
  70.6 2.2 collective-permute-start.7
  72.8 3.3 %collective-permute-start.2 = (f32[16,36,128]{2,1,0:T(8,128)S(1)}, f32[16,36,128]{2,1,0:T(8,128)S(1)}, u32[]{:S(2)}, u32[]{:S(2)}) collective-permute-start(f32[16,36,128]{2,1,0:T(8,128)S(1)} %all-to-all-done.2), channel_id=1, source_target_pairs={{0,96},{32,0},{64,32},{96,64},{1,97},{33,1},{65,33},{97,65},{2,98}... | collective-permute-start | bytes 884744 | tf_op jit(solution)/shard_map/ppermute | solution.py:442
  82.3 7.3 %collective-permute-start.12 = (bf16[128,1024]{1,0:T(8,128)(2,1)}, bf16[128,1024]{1,0:T(8,128)(2,1)}, u32[]{:S(2)}, u32[]{:S(2)}) collective-permute-start(bf16[128,1024]{1,0:T(8,128)(2,1)} %get-tuple-element.86), channel_id=1, source_target_pairs={{0,96},{16,112},{1,97},{17,113},{2,98},{18,114},{3,99},{19,115},{3... | collective-permute-start | bytes 786440 | tf_op jit(solution)/shard_map/ppermute | solution.py:517
  89.6 2.2 collective-permute-start.11
  92.5 2.0 collective-permute-start.10
  94.5 3.6 %pack_rows.1 = bf16[32,4,64,128]{3,2,1,0:T(8,128)(2,1)} custom-call(s32[16]{0:T(128)S(1)} %fusion.26.tab, bf16[2048,512]{1,0:T(8,128)(2,1)S(1)} %copy-done.1, bf16[2048,512]{1,0:T(8,128)(2,1)S(1)} %copy-done.1), custom_call_target="tpu_custom_call" | custom-call | bytes 4194304 | tf_op jit(solution)/shard_map/pack_rows/pallas_call | solution.py:180
  98.2 3.1 %collective-permute-done.10 = bf16[128,1024]{1,0:T(8,128)(2,1)} collective-permute-done((bf16[128,1024]{1,0:T(8,128)(2,1)S(1)}, bf16[128,1024]{1,0:T(8,128)(2,1)}, u32[]{:S(2)}, u32[]{:S(2)}) %collective-permute-start.10) | collective-permute-done | bytes 262176 | tf_op jit(solution)/shard_map/ppermute | solution.py:517
  112.0 6.8 %all-to-all-start.3 = ((bf16[32,4,64,128]{3,2,1,0:T(8,128)(2,1)}), bf16[32,4,64,128]{3,2,1,0:T(8,128)(2,1)S(1)}, u32[]{:S(2)}, u32[]{:S(2)}) async-start(bf16[32,4,64,128]{3,2,1,0:T(8,128)(2,1)} %pack_rows.1), calls=%async_computation.3 | async-start | bytes 4194304 | tf_op jit(solution)/shard_map/all_to_all | solution.py:546
  122.6 22.1 %panel1.1 = (f32[512,512]{1,0:T(8,128)}, bf16[512,512]{1,0:T(8,128)(2,1)}, bf16[512,512]{1,0:T(8,128)(2,1)}) custom-call(f32[36,128,128]{2,1,0:T(8,128)} %bitcast.123), custom_call_target="tpu_custom_call" | custom-call | flops 24999999488 | bytes 4194304 | tf_op jit(solution)/shard_map/panel1/pallas_call | solution.py:158
  144.7 6.8 %all-to-all-done.3 = bf16[32,4,64,128]{3,2,1,0:T(8,128)(2,1)S(1)} async-done(((bf16[32,4,64,128]{3,2,1,0:T(8,128)(2,1)}), bf16[32,4,64,128]{3,2,1,0:T(8,128)(2,1)S(1)}, u32[]{:S(2)}, u32[]{:S(2)}) %all-to-all-start.3) | async-done | bytes 2097184 | tf_op jit(solution)/shard_map/all_to_all | solution.py:546
  152.7 2.0 copy-done
  154.8 7.1 %all-to-all-start.4 = ((bf16[16,8,2,64,128]{4,3,2,1,0:T(8,128)(2,1)}), bf16[16,8,2,64,128]{4,3,2,1,0:T(8,128)(2,1)}, u32[]{:S(2)}, u32[]{:S(2)}) async-start(bf16[16,8,2,64,128]{4,3,2,1,0:T(8,128)(2,1)} %copy-done), calls=%async_computation.4 | async-start | bytes 8388608 | tf_op jit(solution)/shard_map/all_to_all | solution.py:562
  162.6 27.0 %panel2.1 = (bf16[512,512]{1,0:T(8,128)(2,1)}, bf16[512,512]{1,0:T(8,128)(2,1)}, bf16[512,512]{1,0:T(8,128)(2,1)}, bf16[512,512]{1,0:T(8,128)(2,1)}) custom-call(f32[36,128,128]{2,1,0:T(8,128)} %bitcast.124, f32[512,512]{1,0:T(8,128)} %get-tuple-element.60.i1_ref), custom_call_target="tpu_custom_call" | custom-call | flops 24999999488 | bytes 4194304 | tf_op jit(solution)/shard_map/panel2/pallas_call | solution.py:158
  189.5 27.7 %factor_rows.1 = (bf16[3072,1024]{1,0:T(8,128)(2,1)}, bf16[3072,1024]{1,0:T(8,128)(2,1)}, f32[128,1024]{1,0:T(8,128)}) custom-call(s32[297]{0:T(512)} %concatenate.16.tab, bf16[8,48,64,128]{3,2,1,0:T(8,128)(2,1)} %bitcast.141, bf16[2048,1024]{1,0:T(8,128)(2,1)} %own.1, bf16[8,48,64,128]{3,2,1,0:T(8,128)(2,1)} %bitcast.142, ...), custom_call_target="tpu_custom_call" | custom-call | flops 16000000000 | bytes 31457280 | tf_op jit(solution)/shard_map/factor_rows/pallas_call | solution.py:348
  217.2 7.1 %all-to-all-done.4 = bf16[16,8,2,64,128]{4,3,2,1,0:T(8,128)(2,1)} async-done(((bf16[16,8,2,64,128]{4,3,2,1,0:T(8,128)(2,1)}), bf16[16,8,2,64,128]{4,3,2,1,0:T(8,128)(2,1)}, u32[]{:S(2)}, u32[]{:S(2)}) %all-to-all-start.4) | async-done | bytes 4194336 | tf_op jit(solution)/shard_map/all_to_all | solution.py:562
  224.4 21.9 %update.1 = bf16[2048,1024]{1,0:T(8,128)(2,1)} custom-call(s32[177]{0:T(256)} %pad_add_fusion.tab, bf16[3072,1024]{1,0:T(8,128)(2,1)} %get-tuple-element.65.qh.rh, bf16[3072,1024]{1,0:T(8,128)(2,1)} %get-tuple-element.66.ql.rl, bf16[3072,1024]{1,0:T(8,128)(2,1)} %get-tuple-element.65.qh.rh, bf16[3072,1024]{1,0:T(8,128)(2,1)} %get-tuple-element.66.ql.rl, ...), custom_call_target="tpu_custom_call" | custom-call | flops 12999999488 | bytes 37748736 | tf_op jit(solution)/shard_map/update/pallas_call | solution.py:423
  (159 shorter events, 46.9 us)
Async XLA Ops:
  13.1 20.0 %all-to-all-start = ((bf16[32,64,128]{2,1,0:T(8,128)(2,1)}), bf16[32,64,128]{2,1,0:T(8,128)(2,1)S(1)}, u32[]{:S(2)}, u32[]{:S(2)}) async-start(bf16[32,64,128]{2,1,0:T(8,128)(2,1)} %bitcast.21), calls=%async_computation | async-start | bytes 1048576 | tf_op jit(solution)/shard_map/all_to_all | solution.py:482
  21.3 168.2 %all-gather.4.cloned.1.call-start = ((), (), s32[]{:S(2)}) async-start(), calls=%async_computation.5 | async-start | bytes 4456448 | tf_op jit(solution)/shard_map/all_gather | solution.py:502
  29.5 26.6 %copy-start.6 = (s32[36]{0:T(128)S(1)}, s32[36]{0:T(128)}, u32[]{:S(2)}) copy-start(s32[36]{0:T(128)} %constant.399.clone) | copy-start | bytes 436
  35.8 19.4 %all-to-all-start.1 = ((bf16[128,8,128]{2,1,0:T(8,128)(2,1)}), bf16[128,8,128]{2,1,0:T(8,128)(2,1)S(1)}, u32[]{:S(2)}, u32[]{:S(2)}) async-start(bf16[128,8,128]{2,1,0:T(8,128)(2,1)} %copy.69), calls=%async_computation.1 | async-start | bytes 524288 | tf_op jit(solution)/shard_map/all_to_all | solution.py:503
  42.7 33.4 %collective-permute-start.9 = (bf16[4,128,1024]{2,1,0:T(8,128)(2,1)}, bf16[4,128,1024]{2,1,0:T(8,128)(2,1)S(1)}, u32[]{:S(2)}, u32[]{:S(2)}) collective-permute-start(bf16[4,128,1024]{2,1,0:T(8,128)(2,1)} %dynamic-slice_bitcast_fusion), channel_id=1, source_target_pairs={{0,16},{1,17},{18,2},{19,3},{36,52},{37,53},{54,38},{55,39},{72,88... | collective-permute-start | bytes 3145736 | tf_op jit(solution)/shard_map/ppermute | solution.py:505
  49.0 11.6 %collective-permute-start.3 = (bf16[4,2,128,128]{3,2,1,0:T(8,128)(2,1)}, bf16[4,2,128,128]{3,2,1,0:T(8,128)(2,1)S(1)}, u32[]{:S(2)}, u32[]{:S(2)}) collective-permute-start(bf16[4,2,128,128]{3,2,1,0:T(8,128)(2,1)} %get-tuple-element.37), channel_id=1, source_target_pairs={{0,1},{1,2},{2,3},{3,0},{4,5},{5,6},{6,7},{7,4},{8,9},{9,10},{10,1... | collective-permute-start | bytes 786440 | tf_op jit(solution)/shard_map/ppermute | solution.py:442
  50.7 16.1 %collective-permute-start.4 = (bf16[4,2,128,128]{3,2,1,0:T(8,128)(2,1)S(1)}, bf16[4,2,128,128]{3,2,1,0:T(8,128)(2,1)S(1)}, u32[]{:S(2)}, u32[]{:S(2)}) collective-permute-start(bf16[4,2,128,128]{3,2,1,0:T(8,128)(2,1)S(1)} %get-tuple-element.38), channel_id=1, source_target_pairs={{0,2},{1,3},{2,0},{3,1},{4,6},{5,7},{6,4},{7,5},{8,10},{9,11},{10,... | collective-permute-start | bytes 786440 | tf_op jit(solution)/shard_map/ppermute | solution.py:442
  52.6 14.2 %collective-permute-start.5 = (bf16[4,2,128,128]{3,2,1,0:T(8,128)(2,1)S(1)}, bf16[4,2,128,128]{3,2,1,0:T(8,128)(2,1)}, u32[]{:S(2)}, u32[]{:S(2)}) collective-permute-start(bf16[4,2,128,128]{3,2,1,0:T(8,128)(2,1)S(1)} %get-tuple-element.39), channel_id=1, source_target_pairs={{0,3},{1,0},{2,1},{3,2},{4,7},{5,4},{6,5},{7,6},{8,11},{9,8},{10,9... | collective-permute-start | bytes 786440 | tf_op jit(solution)/shard_map/ppermute | solution.py:442
  57.0 15.9 %all-to-all-start.2 = ((f32[16,36,128]{2,1,0:T(8,128)}), f32[16,36,128]{2,1,0:T(8,128)S(1)}, u32[]{:S(2)}, u32[]{:S(2)}) async-start(f32[16,36,128]{2,1,0:T(8,128)} %broadcast_in_dim.146), calls=%async_computation.2 | async-start | bytes 655360 | tf_op jit(solution)/shard_map/all_to_all | solution.py:541
  60.5 129.0 %all-gather.6.cloned.1.call-start = ((), (), s32[]{:S(2)}) async-start(), calls=%async_computation.6 | async-start | bytes 7077888 | tf_op jit(solution)/shard_map/all_gather | solution.py:550
  68.6 9.7 %collective-permute-start.8 = (bf16[2,2,128,128]{3,2,1,0:T(8,128)(2,1)}, bf16[2,2,128,128]{3,2,1,0:T(8,128)(2,1)}, u32[]{:S(2)}, u32[]{:S(2)}) collective-permute-start(bf16[2,2,128,128]{3,2,1,0:T(8,128)(2,1)} %get-tuple-element.92), channel_id=1, source_target_pairs={{0,12},{4,0},{8,4},{12,8},{1,13},{5,1},{9,5},{13,9},{2,14},{6,2},{... | collective-permute-start | bytes 393224 | tf_op jit(solution)/shard_map/ppermute | solution.py:442
  70.6 11.7 %collective-permute-start.6 = (bf16[2,2,128,128]{3,2,1,0:T(8,128)(2,1)}, bf16[2,2,128,128]{3,2,1,0:T(8,128)(2,1)}, u32[]{:S(2)}, u32[]{:S(2)}) collective-permute-start(bf16[2,2,128,128]{3,2,1,0:T(8,128)(2,1)} %get-tuple-element.94), channel_id=1, source_target_pairs={{0,4},{4,8},{8,12},{12,0},{1,5},{5,9},{9,13},{13,1},{2,6},{6,10},{... | collective-permute-start | bytes 393224 | tf_op jit(solution)/shard_map/ppermute | solution.py:442
  70.6 23.9 %copy-start.1 = (bf16[2048,512]{1,0:T(8,128)(2,1)S(1)}, bf16[2048,512]{1,0:T(8,128)(2,1)}, u32[]{:S(2)}) copy-start(bf16[2048,512]{1,0:T(8,128)(2,1)} %low.1) | copy-start | bytes 6291460
  70.6 18.9 %collective-permute-start.7 = (bf16[2,2,128,128]{3,2,1,0:T(8,128)(2,1)}, bf16[2,2,128,128]{3,2,1,0:T(8,128)(2,1)}, u32[]{:S(2)}, u32[]{:S(2)}) collective-permute-start(bf16[2,2,128,128]{3,2,1,0:T(8,128)(2,1)} %get-tuple-element.95), channel_id=1, source_target_pairs={{0,8},{4,12},{8,0},{12,4},{1,9},{5,13},{9,1},{13,5},{2,10},{6,14},... | collective-permute-start | bytes 393224 | tf_op jit(solution)/shard_map/ppermute | solution.py:442
  72.8 19.0 %collective-permute-start.2 = (f32[16,36,128]{2,1,0:T(8,128)S(1)}, f32[16,36,128]{2,1,0:T(8,128)S(1)}, u32[]{:S(2)}, u32[]{:S(2)}) collective-permute-start(f32[16,36,128]{2,1,0:T(8,128)S(1)} %all-to-all-done.2), channel_id=1, source_target_pairs={{0,96},{32,0},{64,32},{96,64},{1,97},{33,1},{65,33},{97,65},{2,98}... | collective-permute-start | bytes 884744 | tf_op jit(solution)/shard_map/ppermute | solution.py:442
  76.1 22.0 %collective-permute-start.1 = (f32[16,36,128]{2,1,0:T(8,128)S(1)}, f32[16,36,128]{2,1,0:T(8,128)}, u32[]{:S(2)}, u32[]{:S(2)}) collective-permute-start(f32[16,36,128]{2,1,0:T(8,128)S(1)} %all-to-all-done.2), channel_id=1, source_target_pairs={{0,64},{32,96},{64,0},{96,32},{1,65},{33,97},{65,1},{97,33},{2,66}... | collective-permute-start | bytes 884744 | tf_op jit(solution)/shard_map/ppermute | solution.py:442
  78.3 19.8 %collective-permute-start = (f32[16,36,128]{2,1,0:T(8,128)S(1)}, f32[16,36,128]{2,1,0:T(8,128)S(1)}, u32[]{:S(2)}, u32[]{:S(2)}) collective-permute-start(f32[16,36,128]{2,1,0:T(8,128)S(1)} %all-to-all-done.2), channel_id=1, source_target_pairs={{0,32},{32,64},{64,96},{96,0},{1,33},{33,65},{65,97},{97,1},{2,34}... | collective-permute-start | bytes 884744 | tf_op jit(solution)/shard_map/ppermute | solution.py:442
  82.3 15.8 %collective-permute-start.12 = (bf16[128,1024]{1,0:T(8,128)(2,1)}, bf16[128,1024]{1,0:T(8,128)(2,1)}, u32[]{:S(2)}, u32[]{:S(2)}) collective-permute-start(bf16[128,1024]{1,0:T(8,128)(2,1)} %get-tuple-element.86), channel_id=1, source_target_pairs={{0,96},{16,112},{1,97},{17,113},{2,98},{18,114},{3,99},{19,115},{3... | collective-permute-start | bytes 786440 | tf_op jit(solution)/shard_map/ppermute | solution.py:517
  89.6 8.6 %collective-permute-start.11 = (bf16[128,1024]{1,0:T(8,128)(2,1)S(1)}, bf16[128,1024]{1,0:T(8,128)(2,1)}, u32[]{:S(2)}, u32[]{:S(2)}) collective-permute-start(bf16[128,1024]{1,0:T(8,128)(2,1)S(1)} %get-tuple-element.87), channel_id=1, source_target_pairs={{0,64},{16,80},{1,65},{17,81},{2,66},{18,82},{3,67},{19,83},{36,10... | collective-permute-start | bytes 786440 | tf_op jit(solution)/shard_map/ppermute | solution.py:517
  92.5 8.7 %collective-permute-start.10 = (bf16[128,1024]{1,0:T(8,128)(2,1)S(1)}, bf16[128,1024]{1,0:T(8,128)(2,1)}, u32[]{:S(2)}, u32[]{:S(2)}) collective-permute-start(bf16[128,1024]{1,0:T(8,128)(2,1)S(1)} %get-tuple-element.88), channel_id=1, source_target_pairs={{0,32},{16,48},{1,33},{17,49},{2,34},{18,50},{3,35},{19,51},{36,68... | collective-permute-start | bytes 786440 | tf_op jit(solution)/shard_map/ppermute | solution.py:517
  98.1 4.4 %copy-start.2 = (bf16[2,2,128,128]{3,2,1,0:T(8,128)(2,1)S(1)}, bf16[2,2,128,128]{3,2,1,0:T(8,128)(2,1)}, u32[]{:S(2)}) copy-start(bf16[2,2,128,128]{3,2,1,0:T(8,128)(2,1)} %get-tuple-element.41) | copy-start | bytes 393220
  109.4 9.4 %collective-permute-start.13 = (f32[4,16,36,128]{3,1,2,0:T(8,128)}, f32[4,16,36,128]{3,1,2,0:T(8,128)}, u32[]{:S(2)}, u32[]{:S(2)}) collective-permute-start(f32[4,16,36,128]{3,1,2,0:T(8,128)} %copy.73), channel_id=1, source_target_pairs={{0,16},{16,0},{1,17},{17,1},{2,18},{18,2},{3,19},{19,3},{4,20},{20... | collective-permute-start | bytes 3538952 | tf_op jit(solution)/shard_map/ppermute | solution.py:446
  112.0 39.5 %all-to-all-start.3 = ((bf16[32,4,64,128]{3,2,1,0:T(8,128)(2,1)}), bf16[32,4,64,128]{3,2,1,0:T(8,128)(2,1)S(1)}, u32[]{:S(2)}, u32[]{:S(2)}) async-start(bf16[32,4,64,128]{3,2,1,0:T(8,128)(2,1)} %pack_rows.1), calls=%async_computation.3 | async-start | bytes 4194304 | tf_op jit(solution)/shard_map/all_to_all | solution.py:546
  154.8 69.6 %all-to-all-start.4 = ((bf16[16,8,2,64,128]{4,3,2,1,0:T(8,128)(2,1)}), bf16[16,8,2,64,128]{4,3,2,1,0:T(8,128)(2,1)}, u32[]{:S(2)}, u32[]{:S(2)}) async-start(bf16[16,8,2,64,128]{4,3,2,1,0:T(8,128)(2,1)} %copy-done), calls=%async_computation.4 | async-start | bytes 8388608 | tf_op jit(solution)/shard_map/all_to_all | solution.py:562
  (4 other events, 11.3 us)
Sparse Core Ops, SparseCore 0:
  34.7 60.7 all-gather.3
  104.8 64.4 all-gather.5

commit v2 on v1

--- a/solution.py
+++ b/solution.py
@@ -539,11 +539,10 @@
     lead = jnp.broadcast_to((lead + lead_own.astype(F32))[None], (16, 36, T))
 
     lead = lax.all_to_all(lead, COL, 0, 0, tiled=True)
+    lead, packed = lax.optimization_barrier((lead, packed))
+    here = lax.all_to_all(packed, ROW + ("x",), 0, 0, tiled=True).reshape(128, 64, T)
     by_shift = [lead] + [shift(lead, "z", k) for k in range(1, 4)]
-    by_shift, along_y, along_z, packed = lax.optimization_barrier(
-        (by_shift, along_y, along_z, packed)
-    )
-    here = lax.all_to_all(packed, ROW + ("x",), 0, 0, tiled=True).reshape(128, 64, T)
+    by_shift, along_y, along_z = lax.optimization_barrier((by_shift, along_y, along_z))
     own_q = jnp.where(z == y, along_z[0], 0) + along_z[1] + along_z[2] + along_z[3]
     own_q = own_q.reshape(2, 64, 8, T).transpose(2, 0, 1, 3).reshape(16, 64, T)
     parts = jnp.concatenate([jnp.stack(along_y).reshape(32, 64, T), own_q], axis=0)

time: 254 us -> 260 us (1.024)
  waiting for transfers between devices: 29.6 us -> 39.9 us
  starting transfers between devices: 60.4 us -> 57.7 us
    all_to_all x1, waiting for transfers between devices: 0.01 us -> 5.37 us  [body(): lead = lax.all_to_all(lead, COL, 0, 0, tiled=True)]
    ppermute x3, waiting for transfers between devices: 3.08 us -> 7.57 us  [body(): lax.ppermute(along_z[k], ALL, [(place(b, c, b, a), place((b + k) % 4, c,...]
    ppermute x9, starting transfers between devices: 14.8 us -> 11.8 us  [shift(): return lax.ppermute(x, axis, [(i, (i + k) % 4) for i in range(4)])]
  transfers between devices with their start and end apart: 21 -> 21, of which waited for: 7 -> 12; matrix products, arithmetic and copies ran while one was open for 12% -> 11% of each run, Pallas kernels for 32% -> 31%
where the time goes in v2:
time: 260 us; the launch traced here: 259 us
  Pallas kernels  104 us (40%)
  starting transfers between devices  57.7 us (22%)
  waiting for transfers between devices  39.9 us (15%)
  local copies, waits for them, and re-layouts  29.5 us (11%)
  between operations  19.6 us (8%)
  other arithmetic  8.61 us (3%)
    pallas_call x2, Pallas kernels, panel_call(): pl.pallas_call(kernel, out_shape=tuple((jax.ShapeDtypeStruct((PW, PW), t)...  49 us
    pallas_call x1, Pallas kernels, factor_rows(): pl.pallas_call(factor_kernel, out_shape=(shape, shape, jax.ShapeDtypeStru...  27.7 us
    pallas_call x1, Pallas kernels, update(): pl.pallas_call(update_kernel, out_shape=jax.ShapeDtypeStruct((2048, 1024)...  21.9 us
    ppermute x9, starting transfers between devices, shift(): return lax.ppermute(x, axis, [(i, (i + k) % 4) for i in range(4)])  11.8 us
    ppermute x3, starting transfers between devices, body(): lax.ppermute(along_z[k], ALL, [(place(b, c, b, a), place((b + k) % 4, c,...  11.1 us
    all_to_all x1, starting transfers between devices, body(): lax.all_to_all(mine.reshape(32, 64, T), ROW + ('x',), 0, 0, tiled=True)  8.24 us
    all_to_all x1, starting transfers between devices, body(): lax.all_to_all(packed, ROW + ('x',), 0, 0, tiled=True).reshape(128, 64, T)  8.18 us
    ppermute x9, waiting for transfers between devices, shift(): return lax.ppermute(x, axis, [(i, (i + k) % 4) for i in range(4)])  7.99 us
  transfers between devices with their start and end apart: 21, of which 12 were waited for; matrix products, arithmetic and copies ran while one was open for 11% of the time, Pallas kernels for 31%

profile of v2, /device:TPU:0, one launch (start us, length us, event | category | flops | bytes accessed | tf_op | source)
XLA Modules:
  0.0 259.1 jit_solution(7172991567833117057)
XLA Ops:
  13.1 8.2 %all-to-all-start = ((bf16[32,64,128]{2,1,0:T(8,128)(2,1)}), bf16[32,64,128]{2,1,0:T(8,128)(2,1)S(1)}, u32[]{:S(2)}, u32[]{:S(2)}) async-start(bf16[32,64,128]{2,1,0:T(8,128)(2,1)} %bitcast.21), calls=%async_computation | async-start | bytes 1048576 | tf_op jit(solution)/shard_map/all_to_all | solution.py:482
  25.2 2.3 dynamic-slice_bitcast_fusion
  27.4 2.2 dynamic-slice_bitcast_fusion.5
  29.8 3.3 %all-to-all-done = bf16[32,64,128]{2,1,0:T(8,128)(2,1)S(1)} async-done(((bf16[32,64,128]{2,1,0:T(8,128)(2,1)}), bf16[32,64,128]{2,1,0:T(8,128)(2,1)S(1)}, u32[]{:S(2)}, u32[]{:S(2)}) %all-to-all-start) | async-done | bytes 524320 | tf_op jit(solution)/shard_map/all_to_all | solution.py:482
  40.5 7.5 %all-to-all-start.1 = ((bf16[128,8,128]{2,1,0:T(8,128)(2,1)}), bf16[128,8,128]{2,1,0:T(8,128)(2,1)}, u32[]{:S(2)}, u32[]{:S(2)}) async-start(bf16[128,8,128]{2,1,0:T(8,128)(2,1)} %copy.69), calls=%async_computation.1 | async-start | bytes 524288 | tf_op jit(solution)/shard_map/all_to_all | solution.py:503
  49.7 3.6 %pack_rows.1 = bf16[32,4,64,128]{3,2,1,0:T(8,128)(2,1)} custom-call(s32[16]{0:T(128)S(1)} %fusion.26.tab, bf16[2048,512]{1,0:T(8,128)(2,1)S(1)} %copy-done.1, bf16[2048,512]{1,0:T(8,128)(2,1)S(1)} %copy-done.1), custom_call_target="tpu_custom_call" | custom-call | bytes 4194304 | tf_op jit(solution)/shard_map/pack_rows/pallas_call | solution.py:180
  63.5 3.5 %all-to-all-start.2 = ((f32[16,36,128]{2,1,0:T(8,128)}), f32[16,36,128]{2,1,0:T(8,128)S(1)}, u32[]{:S(2)}, u32[]{:S(2)}) async-start(f32[16,36,128]{2,1,0:T(8,128)} %broadcast_in_dim.146), calls=%async_computation.2 | async-start | bytes 655360 | tf_op jit(solution)/shard_map/all_to_all | solution.py:541
  67.2 2.5 collective-permute-done.4
  69.6 3.0 %collective-permute-done.5 = bf16[4,2,128,128]{3,2,1,0:T(8,128)(2,1)S(1)} collective-permute-done((bf16[4,2,128,128]{3,2,1,0:T(8,128)(2,1)}, bf16[4,2,128,128]{3,2,1,0:T(8,128)(2,1)S(1)}, u32[]{:S(2)}, u32[]{:S(2)}) %collective-permute-start.5) | collective-permute-done | bytes 262176 | tf_op jit(solution)/shard_map/ppermute | solution.py:442
  75.5 5.4 %all-to-all-done.2 = f32[16,36,128]{2,1,0:T(8,128)S(1)} async-done(((f32[16,36,128]{2,1,0:T(8,128)}), f32[16,36,128]{2,1,0:T(8,128)S(1)}, u32[]{:S(2)}, u32[]{:S(2)}) %all-to-all-start.2) | async-done | bytes 294944 | tf_op jit(solution)/shard_map/all_to_all | solution.py:541
  80.9 3.3 %collective-permute-start.2 = (f32[16,36,128]{2,1,0:T(8,128)S(1)}, f32[16,36,128]{2,1,0:T(8,128)S(1)}, u32[]{:S(2)}, u32[]{:S(2)}) collective-permute-start(f32[16,36,128]{2,1,0:T(8,128)S(1)} %all-to-all-done.2), channel_id=1, source_target_pairs={{0,96},{32,0},{64,32},{96,64},{1,97},{33,1},{65,33},{97,65},{2,98}... | collective-permute-start | bytes 884744 | tf_op jit(solution)/shard_map/ppermute | solution.py:442
  87.1 7.3 %collective-permute-start.12 = (bf16[128,1024]{1,0:T(8,128)(2,1)S(1)}, bf16[128,1024]{1,0:T(8,128)(2,1)S(1)}, u32[]{:S(2)}, u32[]{:S(2)}) collective-permute-start(bf16[128,1024]{1,0:T(8,128)(2,1)S(1)} %get-tuple-element.88), channel_id=1, source_target_pairs={{0,96},{16,112},{1,97},{17,113},{2,98},{18,114},{3,99},{19,115},{3... | collective-permute-start | bytes 786440 | tf_op jit(solution)/shard_map/ppermute | solution.py:517
  94.5 2.5 collective-permute-start.11
  96.9 2.4 collective-permute-done.2
  102.7 2.3 collective-permute-done.11
  105.0 3.3 %collective-permute-done.10 = bf16[128,1024]{1,0:T(8,128)(2,1)S(1)} collective-permute-done((bf16[128,1024]{1,0:T(8,128)(2,1)S(1)}, bf16[128,1024]{1,0:T(8,128)(2,1)S(1)}, u32[]{:S(2)}, u32[]{:S(2)}) %collective-permute-start.10) | collective-permute-done | bytes 262176 | tf_op jit(solution)/shard_map/ppermute | solution.py:517
  117.8 8.2 %all-to-all-start.3 = ((bf16[32,4,64,128]{3,2,1,0:T(8,128)(2,1)}), bf16[32,4,64,128]{3,2,1,0:T(8,128)(2,1)S(1)}, u32[]{:S(2)}, u32[]{:S(2)}) async-start(bf16[32,4,64,128]{3,2,1,0:T(8,128)(2,1)} %pack_rows.1), calls=%async_computation.3 | async-start | bytes 4194304 | tf_op jit(solution)/shard_map/all_to_all | solution.py:543
  129.7 22.1 %panel1.1 = (f32[512,512]{1,0:T(8,128)}, bf16[512,512]{1,0:T(8,128)(2,1)}, bf16[512,512]{1,0:T(8,128)(2,1)}) custom-call(f32[36,128,128]{2,1,0:T(8,128)} %bitcast.123), custom_call_target="tpu_custom_call" | custom-call | flops 24999999488 | bytes 4194304 | tf_op jit(solution)/shard_map/panel1/pallas_call | solution.py:158
  151.8 6.8 %all-to-all-done.3 = bf16[32,4,64,128]{3,2,1,0:T(8,128)(2,1)S(1)} async-done(((bf16[32,4,64,128]{3,2,1,0:T(8,128)(2,1)}), bf16[32,4,64,128]{3,2,1,0:T(8,128)(2,1)S(1)}, u32[]{:S(2)}, u32[]{:S(2)}) %all-to-all-start.3) | async-done | bytes 2097184 | tf_op jit(solution)/shard_map/all_to_all | solution.py:543
  161.9 5.9 %all-to-all-start.4 = ((bf16[16,8,2,64,128]{4,3,2,1,0:T(8,128)(2,1)}), bf16[16,8,2,64,128]{4,3,2,1,0:T(8,128)(2,1)}, u32[]{:S(2)}, u32[]{:S(2)}) async-start(bf16[16,8,2,64,128]{4,3,2,1,0:T(8,128)(2,1)} %copy-done), calls=%async_computation.4 | async-start | bytes 8388608 | tf_op jit(solution)/shard_map/all_to_all | solution.py:561
  168.5 26.9 %panel2.1 = (bf16[512,512]{1,0:T(8,128)(2,1)}, bf16[512,512]{1,0:T(8,128)(2,1)}, bf16[512,512]{1,0:T(8,128)(2,1)}, bf16[512,512]{1,0:T(8,128)(2,1)}) custom-call(f32[36,128,128]{2,1,0:T(8,128)} %bitcast.124, f32[512,512]{1,0:T(8,128)} %get-tuple-element.62.i1_ref), custom_call_target="tpu_custom_call" | custom-call | flops 24999999488 | bytes 4194304 | tf_op jit(solution)/shard_map/panel2/pallas_call | solution.py:158
  195.5 27.7 %factor_rows.1 = (bf16[3072,1024]{1,0:T(8,128)(2,1)}, bf16[3072,1024]{1,0:T(8,128)(2,1)}, f32[128,1024]{1,0:T(8,128)}) custom-call(s32[297]{0:T(512)} %concatenate.16.tab, bf16[8,48,64,128]{3,2,1,0:T(8,128)(2,1)} %bitcast.143, bf16[2048,1024]{1,0:T(8,128)(2,1)} %own.1, bf16[8,48,64,128]{3,2,1,0:T(8,128)(2,1)} %bitcast.144, ...), custom_call_target="tpu_custom_call" | custom-call | flops 16000000000 | bytes 31457280 | tf_op jit(solution)/shard_map/factor_rows/pallas_call | solution.py:348
  223.2 7.2 %all-to-all-done.4 = bf16[16,8,2,64,128]{4,3,2,1,0:T(8,128)(2,1)} async-done(((bf16[16,8,2,64,128]{4,3,2,1,0:T(8,128)(2,1)}), bf16[16,8,2,64,128]{4,3,2,1,0:T(8,128)(2,1)}, u32[]{:S(2)}, u32[]{:S(2)}) %all-to-all-start.4) | async-done | bytes 4194336 | tf_op jit(solution)/shard_map/all_to_all | solution.py:561
  230.3 21.9 %update.1 = bf16[2048,1024]{1,0:T(8,128)(2,1)} custom-call(s32[177]{0:T(256)} %pad_add_fusion.tab, bf16[3072,1024]{1,0:T(8,128)(2,1)} %get-tuple-element.67.qh.rh, bf16[3072,1024]{1,0:T(8,128)(2,1)} %get-tuple-element.68.ql.rl, bf16[3072,1024]{1,0:T(8,128)(2,1)} %get-tuple-element.67.qh.rh, bf16[3072,1024]{1,0:T(8,128)(2,1)} %get-tuple-element.68.ql.rl, ...), custom_call_target="tpu_custom_call" | custom-call | flops 12999999488 | bytes 37748736 | tf_op jit(solution)/shard_map/update/pallas_call | solution.py:423
  (153 shorter events, 50.1 us)
Async XLA Ops:
  13.1 20.0 %all-to-all-start = ((bf16[32,64,128]{2,1,0:T(8,128)(2,1)}), bf16[32,64,128]{2,1,0:T(8,128)(2,1)S(1)}, u32[]{:S(2)}, u32[]{:S(2)}) async-start(bf16[32,64,128]{2,1,0:T(8,128)(2,1)} %bitcast.21), calls=%async_computation | async-start | bytes 1048576 | tf_op jit(solution)/shard_map/all_to_all | solution.py:482
  21.3 174.1 %all-gather.4.cloned.1.call-start = ((), (), s32[]{:S(2)}) async-start(), calls=%async_computation.5 | async-start | bytes 4456448 | tf_op jit(solution)/shard_map/all_gather | solution.py:502
  27.4 22.3 %copy-start.1 = (bf16[2048,512]{1,0:T(8,128)(2,1)S(1)}, bf16[2048,512]{1,0:T(8,128)(2,1)}, u32[]{:S(2)}) copy-start(bf16[2048,512]{1,0:T(8,128)(2,1)} %low.1) | copy-start | bytes 6291460
  40.5 19.5 %all-to-all-start.1 = ((bf16[128,8,128]{2,1,0:T(8,128)(2,1)}), bf16[128,8,128]{2,1,0:T(8,128)(2,1)}, u32[]{:S(2)}, u32[]{:S(2)}) async-start(bf16[128,8,128]{2,1,0:T(8,128)(2,1)} %copy.69), calls=%async_computation.1 | async-start | bytes 524288 | tf_op jit(solution)/shard_map/all_to_all | solution.py:503
  48.1 36.1 %collective-permute-start.9 = (bf16[4,128,1024]{2,1,0:T(8,128)(2,1)}, bf16[4,128,1024]{2,1,0:T(8,128)(2,1)S(1)}, u32[]{:S(2)}, u32[]{:S(2)}) collective-permute-start(bf16[4,128,1024]{2,1,0:T(8,128)(2,1)} %dynamic-slice_bitcast_fusion), channel_id=1, source_target_pairs={{0,16},{1,17},{18,2},{19,3},{36,52},{37,53},{54,38},{55,39},{72,88... | collective-permute-start | bytes 3145736 | tf_op jit(solution)/shard_map/ppermute | solution.py:505
  49.7 12.9 %copy-start.3 = (s32[36]{0:T(128)S(1)}, s32[36]{0:T(128)}, u32[]{:S(2)}) copy-start(s32[36]{0:T(128)} %constant.399.clone) | copy-start | bytes 436
  53.3 13.8 %collective-permute-start.3 = (bf16[4,2,128,128]{3,2,1,0:T(8,128)(2,1)}, bf16[4,2,128,128]{3,2,1,0:T(8,128)(2,1)S(1)}, u32[]{:S(2)}, u32[]{:S(2)}) collective-permute-start(bf16[4,2,128,128]{3,2,1,0:T(8,128)(2,1)} %get-tuple-element.39), channel_id=1, source_target_pairs={{0,1},{1,2},{2,3},{3,0},{4,5},{5,6},{6,7},{7,4},{8,9},{9,10},{10,1... | collective-permute-start | bytes 786440 | tf_op jit(solution)/shard_map/ppermute | solution.py:442
  55.0 14.6 %collective-permute-start.4 = (bf16[4,2,128,128]{3,2,1,0:T(8,128)(2,1)}, bf16[4,2,128,128]{3,2,1,0:T(8,128)(2,1)S(1)}, u32[]{:S(2)}, u32[]{:S(2)}) collective-permute-start(bf16[4,2,128,128]{3,2,1,0:T(8,128)(2,1)} %get-tuple-element.40), channel_id=1, source_target_pairs={{0,2},{1,3},{2,0},{3,1},{4,6},{5,7},{6,4},{7,5},{8,10},{9,11},{10,... | collective-permute-start | bytes 786440 | tf_op jit(solution)/shard_map/ppermute | solution.py:442
  56.8 15.8 %collective-permute-start.5 = (bf16[4,2,128,128]{3,2,1,0:T(8,128)(2,1)}, bf16[4,2,128,128]{3,2,1,0:T(8,128)(2,1)S(1)}, u32[]{:S(2)}, u32[]{:S(2)}) collective-permute-start(bf16[4,2,128,128]{3,2,1,0:T(8,128)(2,1)} %get-tuple-element.41), channel_id=1, source_target_pairs={{0,3},{1,0},{2,1},{3,2},{4,7},{5,4},{6,5},{7,6},{8,11},{9,8},{10,9... | collective-permute-start | bytes 786440 | tf_op jit(solution)/shard_map/ppermute | solution.py:442
  63.5 17.3 %all-to-all-start.2 = ((f32[16,36,128]{2,1,0:T(8,128)}), f32[16,36,128]{2,1,0:T(8,128)S(1)}, u32[]{:S(2)}, u32[]{:S(2)}) async-start(f32[16,36,128]{2,1,0:T(8,128)} %broadcast_in_dim.146), calls=%async_computation.2 | async-start | bytes 655360 | tf_op jit(solution)/shard_map/all_to_all | solution.py:541
  67.1 128.4 %all-gather.6.cloned.1.call-start = ((), (), s32[]{:S(2)}) async-start(), calls=%async_computation.6 | async-start | bytes 7077888 | tf_op jit(solution)/shard_map/all_gather | solution.py:549
  73.5 12.0 %collective-permute-start.8 = (bf16[2,2,128,128]{3,2,1,0:T(8,128)(2,1)S(1)}, bf16[2,2,128,128]{3,2,1,0:T(8,128)(2,1)S(1)}, u32[]{:S(2)}, u32[]{:S(2)}) collective-permute-start(bf16[2,2,128,128]{3,2,1,0:T(8,128)(2,1)S(1)} %get-tuple-element.94), channel_id=1, source_target_pairs={{0,12},{4,0},{8,4},{12,8},{1,13},{5,1},{9,5},{13,9},{2,14},{6,2},{... | collective-permute-start | bytes 393224 | tf_op jit(solution)/shard_map/ppermute | solution.py:442
  73.5 13.7 %collective-permute-start.6 = (bf16[2,2,128,128]{3,2,1,0:T(8,128)(2,1)}, bf16[2,2,128,128]{3,2,1,0:T(8,128)(2,1)S(1)}, u32[]{:S(2)}, u32[]{:S(2)}) collective-permute-start(bf16[2,2,128,128]{3,2,1,0:T(8,128)(2,1)} %get-tuple-element.96), channel_id=1, source_target_pairs={{0,4},{4,8},{8,12},{12,0},{1,5},{5,9},{9,13},{13,1},{2,6},{6,10},{... | collective-permute-start | bytes 393224 | tf_op jit(solution)/shard_map/ppermute | solution.py:442
  75.5 19.0 %collective-permute-start.7 = (bf16[2,2,128,128]{3,2,1,0:T(8,128)(2,1)}, bf16[2,2,128,128]{3,2,1,0:T(8,128)(2,1)}, u32[]{:S(2)}, u32[]{:S(2)}) collective-permute-start(bf16[2,2,128,128]{3,2,1,0:T(8,128)(2,1)} %get-tuple-element.97), channel_id=1, source_target_pairs={{0,8},{4,12},{8,0},{12,4},{1,9},{5,13},{9,1},{13,5},{2,10},{6,14},... | collective-permute-start | bytes 393224 | tf_op jit(solution)/shard_map/ppermute | solution.py:442
  80.9 18.5 %collective-permute-start.2 = (f32[16,36,128]{2,1,0:T(8,128)S(1)}, f32[16,36,128]{2,1,0:T(8,128)S(1)}, u32[]{:S(2)}, u32[]{:S(2)}) collective-permute-start(f32[16,36,128]{2,1,0:T(8,128)S(1)} %all-to-all-done.2), channel_id=1, source_target_pairs={{0,96},{32,0},{64,32},{96,64},{1,97},{33,1},{65,33},{97,65},{2,98}... | collective-permute-start | bytes 884744 | tf_op jit(solution)/shard_map/ppermute | solution.py:442
  84.2 16.5 %collective-permute-start.1 = (f32[16,36,128]{2,1,0:T(8,128)S(1)}, f32[16,36,128]{2,1,0:T(8,128)}, u32[]{:S(2)}, u32[]{:S(2)}) collective-permute-start(f32[16,36,128]{2,1,0:T(8,128)S(1)} %all-to-all-done.2), channel_id=1, source_target_pairs={{0,64},{32,96},{64,0},{96,32},{1,65},{33,97},{65,1},{97,33},{2,66}... | collective-permute-start | bytes 884744 | tf_op jit(solution)/shard_map/ppermute | solution.py:442
  85.5 15.3 %collective-permute-start = (f32[16,36,128]{2,1,0:T(8,128)S(1)}, f32[16,36,128]{2,1,0:T(8,128)S(1)}, u32[]{:S(2)}, u32[]{:S(2)}) collective-permute-start(f32[16,36,128]{2,1,0:T(8,128)S(1)} %all-to-all-done.2), channel_id=1, source_target_pairs={{0,32},{32,64},{64,96},{96,0},{1,33},{33,65},{65,97},{97,1},{2,34}... | collective-permute-start | bytes 884744 | tf_op jit(solution)/shard_map/ppermute | solution.py:442
  87.1 15.6 %collective-permute-start.12 = (bf16[128,1024]{1,0:T(8,128)(2,1)S(1)}, bf16[128,1024]{1,0:T(8,128)(2,1)S(1)}, u32[]{:S(2)}, u32[]{:S(2)}) collective-permute-start(bf16[128,1024]{1,0:T(8,128)(2,1)S(1)} %get-tuple-element.88), channel_id=1, source_target_pairs={{0,96},{16,112},{1,97},{17,113},{2,98},{18,114},{3,99},{19,115},{3... | collective-permute-start | bytes 786440 | tf_op jit(solution)/shard_map/ppermute | solution.py:517
  94.5 10.6 %collective-permute-start.11 = (bf16[128,1024]{1,0:T(8,128)(2,1)S(1)}, bf16[128,1024]{1,0:T(8,128)(2,1)S(1)}, u32[]{:S(2)}, u32[]{:S(2)}) collective-permute-start(bf16[128,1024]{1,0:T(8,128)(2,1)S(1)} %get-tuple-element.89), channel_id=1, source_target_pairs={{0,64},{16,80},{1,65},{17,81},{2,66},{18,82},{3,67},{19,83},{36,10... | collective-permute-start | bytes 786440 | tf_op jit(solution)/shard_map/ppermute | solution.py:517
  99.4 9.0 %collective-permute-start.10 = (bf16[128,1024]{1,0:T(8,128)(2,1)S(1)}, bf16[128,1024]{1,0:T(8,128)(2,1)S(1)}, u32[]{:S(2)}, u32[]{:S(2)}) collective-permute-start(bf16[128,1024]{1,0:T(8,128)(2,1)S(1)} %get-tuple-element.90), channel_id=1, source_target_pairs={{0,32},{16,48},{1,33},{17,49},{2,34},{18,50},{3,35},{19,51},{36,68... | collective-permute-start | bytes 786440 | tf_op jit(solution)/shard_map/ppermute | solution.py:517
  108.4 4.0 %copy-start.2 = (s32[2,64]{1,0:T(2,128)S(1)}, s32[2,64]{1,0:T(2,128)}, u32[]{:S(2)}) copy-start(s32[2,64]{1,0:T(2,128)} %param.6) | copy-start | bytes 1540
  115.2 10.8 %collective-permute-start.13 = (f32[4,16,36,128]{3,1,2,0:T(8,128)}, f32[4,16,36,128]{3,1,2,0:T(8,128)}, u32[]{:S(2)}, u32[]{:S(2)}) collective-permute-start(f32[4,16,36,128]{3,1,2,0:T(8,128)} %copy.73), channel_id=1, source_target_pairs={{0,16},{16,0},{1,17},{17,1},{2,18},{18,2},{3,19},{19,3},{4,20},{20... | collective-permute-start | bytes 3538952 | tf_op jit(solution)/shard_map/ppermute | solution.py:446
  117.8 40.8 %all-to-all-start.3 = ((bf16[32,4,64,128]{3,2,1,0:T(8,128)(2,1)}), bf16[32,4,64,128]{3,2,1,0:T(8,128)(2,1)S(1)}, u32[]{:S(2)}, u32[]{:S(2)}) async-start(bf16[32,4,64,128]{3,2,1,0:T(8,128)(2,1)} %pack_rows.1), calls=%async_computation.3 | async-start | bytes 4194304 | tf_op jit(solution)/shard_map/all_to_all | solution.py:543
  161.9 68.4 %all-to-all-start.4 = ((bf16[16,8,2,64,128]{4,3,2,1,0:T(8,128)(2,1)}), bf16[16,8,2,64,128]{4,3,2,1,0:T(8,128)(2,1)}, u32[]{:S(2)}, u32[]{:S(2)}) async-start(bf16[16,8,2,64,128]{4,3,2,1,0:T(8,128)(2,1)} %copy-done), calls=%async_computation.4 | async-start | bytes 8388608 | tf_op jit(solution)/shard_map/all_to_all | solution.py:561
  (1 other events, 2.0 us)
Sparse Core Ops, SparseCore 0:
  34.6 61.1 all-gather.3
  110.6 64.6 all-gather.5

commit v3 on v1

--- a/solution.py
+++ b/solution.py
@@ -163,7 +163,7 @@
         + [whole] * len(args),
         out_specs=[whole] * len(outs),
         scratch_shapes=[pltpu.VMEM(x, F32) for x in scratch],
-        compiler_params=pltpu.CompilerParams(vmem_limit_bytes=VMEM),
+        compiler_params=pltpu.CompilerParams(vmem_limit_bytes=24 * MIB),
         cost_estimate=pl.CostEstimate(flops=25 * 10**9, bytes_accessed=4 * MIB, transcendentals=0),
         name=name,
     )(lead, *args)

time: 254 us -> 254 us (level)
  Pallas kernels: 104 us -> 98.3 us
  local copies, waits for them, and re-layouts: 29 us -> 33.9 us
    unnamed x15 -> x31, local copies, waits for them, and re-layouts: 2.8 us -> 9.09 us
    pallas_call x2, Pallas kernels: 49.1 us -> 43.8 us  [panel_call(): pl.pallas_call(kernel, out_shape=tuple((jax.ShapeDtypeStruct((PW, PW), t)...]
  transfers between devices with their start and end apart: 21 -> 21, of which waited for: 7 -> 7; matrix products, arithmetic and copies ran while one was open for 12% -> 12% of each run, Pallas kernels for 32% -> 30%
where the time goes in v3:
time: 254 us; the launch traced here: 253 us
  Pallas kernels  98.3 us (39%)
  starting transfers between devices  60.6 us (24%)
  local copies, waits for them, and re-layouts  33.9 us (13%)
  waiting for transfers between devices  30.1 us (12%)
  between operations  19.3 us (8%)
  other arithmetic  10.9 us (4%)
    pallas_call x2, Pallas kernels, panel_call(): pl.pallas_call(kernel, out_shape=tuple((jax.ShapeDtypeStruct((PW, PW), t)...  43.8 us
    pallas_call x1, Pallas kernels, factor_rows(): pl.pallas_call(factor_kernel, out_shape=(shape, shape, jax.ShapeDtypeStru...  27.6 us
    pallas_call x1, Pallas kernels, update(): pl.pallas_call(update_kernel, out_shape=jax.ShapeDtypeStruct((2048, 1024)...  21.9 us
    ppermute x9, starting transfers between devices, shift(): return lax.ppermute(x, axis, [(i, (i + k) % 4) for i in range(4)])  14.8 us
    ppermute x3, starting transfers between devices, body(): lax.ppermute(along_z[k], ALL, [(place(b, c, b, a), place((b + k) % 4, c,...  11.5 us
    unnamed x31, local copies, waits for them, and re-layouts  9.09 us
    all_to_all x1, starting transfers between devices, body(): lax.all_to_all(mine.reshape(32, 64, T), ROW + ('x',), 0, 0, tiled=True)  8.24 us
    ppermute x9, waiting for transfers between devices, shift(): return lax.ppermute(x, axis, [(i, (i + k) % 4) for i in range(4)])  7.94 us
  transfers between devices with their start and end apart: 21, of which 7 were waited for; matrix products, arithmetic and copies ran while one was open for 12% of the time, Pallas kernels for 30%

profile of v3, /device:TPU:0, one launch (start us, length us, event | category | flops | bytes accessed | tf_op | source)
XLA Modules:
  0.0 253.3 jit_solution(867376791311793124)
XLA Ops:
  13.1 8.2 %all-to-all-start = ((bf16[32,64,128]{2,1,0:T(8,128)(2,1)}), bf16[32,64,128]{2,1,0:T(8,128)(2,1)S(1)}, u32[]{:S(2)}, u32[]{:S(2)}) async-start(bf16[32,64,128]{2,1,0:T(8,128)(2,1)} %bitcast.21), calls=%async_computation | async-start | bytes 1048576 | tf_op jit(solution)/shard_map/all_to_all | solution.py:482
  25.2 2.3 dynamic-slice_bitcast_fusion
  27.4 2.0 dynamic-slice_bitcast_fusion.5
  29.6 3.5 %all-to-all-done = bf16[32,64,128]{2,1,0:T(8,128)(2,1)S(1)} async-done(((bf16[32,64,128]{2,1,0:T(8,128)(2,1)}), bf16[32,64,128]{2,1,0:T(8,128)(2,1)S(1)}, u32[]{:S(2)}, u32[]{:S(2)}) %all-to-all-start) | async-done | bytes 524320 | tf_op jit(solution)/shard_map/all_to_all | solution.py:482
  35.7 6.9 %all-to-all-start.1 = ((bf16[128,8,128]{2,1,0:T(8,128)(2,1)}), bf16[128,8,128]{2,1,0:T(8,128)(2,1)S(1)}, u32[]{:S(2)}, u32[]{:S(2)}) async-start(bf16[128,8,128]{2,1,0:T(8,128)(2,1)} %copy.69), calls=%async_computation.1 | async-start | bytes 524288 | tf_op jit(solution)/shard_map/all_to_all | solution.py:503
  56.9 3.5 %all-to-all-start.2 = ((f32[16,36,128]{2,1,0:T(8,128)}), f32[16,36,128]{2,1,0:T(8,128)S(1)}, u32[]{:S(2)}, u32[]{:S(2)}) async-start(f32[16,36,128]{2,1,0:T(8,128)} %broadcast_in_dim.146), calls=%async_computation.2 | async-start | bytes 655360 | tf_op jit(solution)/shard_map/all_to_all | solution.py:541
  60.6 6.1 %collective-permute-done.4 = bf16[4,2,128,128]{3,2,1,0:T(8,128)(2,1)S(1)} collective-permute-done((bf16[4,2,128,128]{3,2,1,0:T(8,128)(2,1)S(1)}, bf16[4,2,128,128]{3,2,1,0:T(8,128)(2,1)S(1)}, u32[]{:S(2)}, u32[]{:S(2)}) %collective-permute-start.4) | collective-permute-done | bytes 262176 | tf_op jit(solution)/shard_map/ppermute | solution.py:442
  68.6 2.0 collective-permute-start.8
  70.6 2.2 collective-permute-start.7
  72.8 3.3 %collective-permute-start.2 = (f32[16,36,128]{2,1,0:T(8,128)S(1)}, f32[16,36,128]{2,1,0:T(8,128)S(1)}, u32[]{:S(2)}, u32[]{:S(2)}) collective-permute-start(f32[16,36,128]{2,1,0:T(8,128)S(1)} %all-to-all-done.2), channel_id=1, source_target_pairs={{0,96},{32,0},{64,32},{96,64},{1,97},{33,1},{65,33},{97,65},{2,98}... | collective-permute-start | bytes 884744 | tf_op jit(solution)/shard_map/ppermute | solution.py:442
  82.3 7.3 %collective-permute-start.12 = (bf16[128,1024]{1,0:T(8,128)(2,1)}, bf16[128,1024]{1,0:T(8,128)(2,1)}, u32[]{:S(2)}, u32[]{:S(2)}) collective-permute-start(bf16[128,1024]{1,0:T(8,128)(2,1)} %get-tuple-element.86), channel_id=1, source_target_pairs={{0,96},{16,112},{1,97},{17,113},{2,98},{18,114},{3,99},{19,115},{3... | collective-permute-start | bytes 786440 | tf_op jit(solution)/shard_map/ppermute | solution.py:517
  89.5 2.2 collective-permute-start.11
  92.5 2.0 collective-permute-start.10
  94.5 3.6 %pack_rows.1 = bf16[32,4,64,128]{3,2,1,0:T(8,128)(2,1)} custom-call(s32[16]{0:T(128)S(1)} %fusion.26.tab, bf16[2048,512]{1,0:T(8,128)(2,1)S(1)} %copy-done.1, bf16[2048,512]{1,0:T(8,128)(2,1)S(1)} %copy-done.1), custom_call_target="tpu_custom_call" | custom-call | bytes 4194304 | tf_op jit(solution)/shard_map/pack_rows/pallas_call | solution.py:180
  98.1 3.1 %collective-permute-done.10 = bf16[128,1024]{1,0:T(8,128)(2,1)} collective-permute-done((bf16[128,1024]{1,0:T(8,128)(2,1)S(1)}, bf16[128,1024]{1,0:T(8,128)(2,1)}, u32[]{:S(2)}, u32[]{:S(2)}) %collective-permute-start.10) | collective-permute-done | bytes 262176 | tf_op jit(solution)/shard_map/ppermute | solution.py:517
  112.0 6.8 %all-to-all-start.3 = ((bf16[32,4,64,128]{3,2,1,0:T(8,128)(2,1)}), bf16[32,4,64,128]{3,2,1,0:T(8,128)(2,1)S(1)}, u32[]{:S(2)}, u32[]{:S(2)}) async-start(bf16[32,4,64,128]{3,2,1,0:T(8,128)(2,1)} %pack_rows.1), calls=%async_computation.3 | async-start | bytes 4194304 | tf_op jit(solution)/shard_map/all_to_all | solution.py:546
  121.1 20.0 %panel1.1 = (f32[512,512]{1,0:T(8,128)S(1)}, bf16[512,512]{1,0:T(8,128)(2,1)S(1)}, bf16[512,512]{1,0:T(8,128)(2,1)S(1)}) custom-call(f32[36,128,128]{2,1,0:T(8,128)S(1)} %bitcast.120), custom_call_target="tpu_custom_call" | custom-call | flops 24999999488 | bytes 4194304 | tf_op jit(solution)/shard_map/panel1/pallas_call | solution.py:158
  144.1 7.3 %all-to-all-done.3 = bf16[32,4,64,128]{3,2,1,0:T(8,128)(2,1)S(1)} async-done(((bf16[32,4,64,128]{3,2,1,0:T(8,128)(2,1)}), bf16[32,4,64,128]{3,2,1,0:T(8,128)(2,1)S(1)}, u32[]{:S(2)}, u32[]{:S(2)}) %all-to-all-start.3) | async-done | bytes 2097184 | tf_op jit(solution)/shard_map/all_to_all | solution.py:546
  152.7 2.0 copy-done
  154.7 7.4 %all-to-all-start.4 = ((bf16[16,8,2,64,128]{4,3,2,1,0:T(8,128)(2,1)}), bf16[16,8,2,64,128]{4,3,2,1,0:T(8,128)(2,1)}, u32[]{:S(2)}, u32[]{:S(2)}) async-start(bf16[16,8,2,64,128]{4,3,2,1,0:T(8,128)(2,1)} %copy-done), calls=%async_computation.4 | async-start | bytes 8388608 | tf_op jit(solution)/shard_map/all_to_all | solution.py:562
  162.7 23.9 %panel2.1 = (bf16[512,512]{1,0:T(8,128)(2,1)S(1)}, bf16[512,512]{1,0:T(8,128)(2,1)S(1)}, bf16[512,512]{1,0:T(8,128)(2,1)S(1)}, bf16[512,512]{1,0:T(8,128)(2,1)S(1)}) custom-call(f32[36,128,128]{2,1,0:T(8,128)S(1)} %bitcast.121, f32[512,512]{1,0:T(8,128)S(1)} %get-tuple-element.60.i1_ref), custom_call_target="tpu_custom_call" | custom-call | flops 24999999488 | bytes 4194304 | tf_op jit(solution)/shard_map/panel2/pallas_call | solution.py:158
  189.8 27.6 %factor_rows.1 = (bf16[3072,1024]{1,0:T(8,128)(2,1)}, bf16[3072,1024]{1,0:T(8,128)(2,1)}, f32[128,1024]{1,0:T(8,128)}) custom-call(s32[297]{0:T(512)} %concatenate.16.tab, bf16[8,48,64,128]{3,2,1,0:T(8,128)(2,1)} %bitcast.141, bf16[2048,1024]{1,0:T(8,128)(2,1)} %own.1, bf16[8,48,64,128]{3,2,1,0:T(8,128)(2,1)} %bitcast.142, ...), custom_call_target="tpu_custom_call" | custom-call | flops 16000000000 | bytes 31457280 | tf_op jit(solution)/shard_map/factor_rows/pallas_call | solution.py:348
  217.4 7.1 %all-to-all-done.4 = bf16[16,8,2,64,128]{4,3,2,1,0:T(8,128)(2,1)} async-done(((bf16[16,8,2,64,128]{4,3,2,1,0:T(8,128)(2,1)}), bf16[16,8,2,64,128]{4,3,2,1,0:T(8,128)(2,1)}, u32[]{:S(2)}, u32[]{:S(2)}) %all-to-all-start.4) | async-done | bytes 4194336 | tf_op jit(solution)/shard_map/all_to_all | solution.py:562
  224.5 21.9 %update.1 = bf16[2048,1024]{1,0:T(8,128)(2,1)} custom-call(s32[177]{0:T(256)} %pad_add_fusion.tab, bf16[3072,1024]{1,0:T(8,128)(2,1)} %get-tuple-element.65.qh.rh, bf16[3072,1024]{1,0:T(8,128)(2,1)} %get-tuple-element.66.ql.rl, bf16[3072,1024]{1,0:T(8,128)(2,1)} %get-tuple-element.65.qh.rh, bf16[3072,1024]{1,0:T(8,128)(2,1)} %get-tuple-element.66.ql.rl, ...), custom_call_target="tpu_custom_call" | custom-call | flops 12999999488 | bytes 37748736 | tf_op jit(solution)/shard_map/update/pallas_call | solution.py:423
  (175 shorter events, 51.8 us)
Async XLA Ops:
  13.1 20.0 %all-to-all-start = ((bf16[32,64,128]{2,1,0:T(8,128)(2,1)}), bf16[32,64,128]{2,1,0:T(8,128)(2,1)S(1)}, u32[]{:S(2)}, u32[]{:S(2)}) async-start(bf16[32,64,128]{2,1,0:T(8,128)(2,1)} %bitcast.21), calls=%async_computation | async-start | bytes 1048576 | tf_op jit(solution)/shard_map/all_to_all | solution.py:482
  21.3 168.5 %all-gather.4.cloned.1.call-start = ((), (), s32[]{:S(2)}) async-start(), calls=%async_computation.5 | async-start | bytes 4456448 | tf_op jit(solution)/shard_map/all_gather | solution.py:502
  29.5 26.5 %copy-start.14 = (s32[36]{0:T(128)S(1)}, s32[36]{0:T(128)}, u32[]{:S(2)}) copy-start(s32[36]{0:T(128)} %constant.399.clone) | copy-start | bytes 436
  35.7 19.4 %all-to-all-start.1 = ((bf16[128,8,128]{2,1,0:T(8,128)(2,1)}), bf16[128,8,128]{2,1,0:T(8,128)(2,1)S(1)}, u32[]{:S(2)}, u32[]{:S(2)}) async-start(bf16[128,8,128]{2,1,0:T(8,128)(2,1)} %copy.69), calls=%async_computation.1 | async-start | bytes 524288 | tf_op jit(solution)/shard_map/all_to_all | solution.py:503
  42.7 33.4 %collective-permute-start.9 = (bf16[4,128,1024]{2,1,0:T(8,128)(2,1)}, bf16[4,128,1024]{2,1,0:T(8,128)(2,1)S(1)}, u32[]{:S(2)}, u32[]{:S(2)}) collective-permute-start(bf16[4,128,1024]{2,1,0:T(8,128)(2,1)} %dynamic-slice_bitcast_fusion), channel_id=1, source_target_pairs={{0,16},{1,17},{18,2},{19,3},{36,52},{37,53},{54,38},{55,39},{72,88... | collective-permute-start | bytes 3145736 | tf_op jit(solution)/shard_map/ppermute | solution.py:505
  48.9 11.6 %collective-permute-start.3 = (bf16[4,2,128,128]{3,2,1,0:T(8,128)(2,1)}, bf16[4,2,128,128]{3,2,1,0:T(8,128)(2,1)S(1)}, u32[]{:S(2)}, u32[]{:S(2)}) collective-permute-start(bf16[4,2,128,128]{3,2,1,0:T(8,128)(2,1)} %get-tuple-element.37), channel_id=1, source_target_pairs={{0,1},{1,2},{2,3},{3,0},{4,5},{5,6},{6,7},{7,4},{8,9},{9,10},{10,1... | collective-permute-start | bytes 786440 | tf_op jit(solution)/shard_map/ppermute | solution.py:442
  50.7 16.0 %collective-permute-start.4 = (bf16[4,2,128,128]{3,2,1,0:T(8,128)(2,1)S(1)}, bf16[4,2,128,128]{3,2,1,0:T(8,128)(2,1)S(1)}, u32[]{:S(2)}, u32[]{:S(2)}) collective-permute-start(bf16[4,2,128,128]{3,2,1,0:T(8,128)(2,1)S(1)} %get-tuple-element.38), channel_id=1, source_target_pairs={{0,2},{1,3},{2,0},{3,1},{4,6},{5,7},{6,4},{7,5},{8,10},{9,11},{10,... | collective-permute-start | bytes 786440 | tf_op jit(solution)/shard_map/ppermute | solution.py:442
  52.5 14.2 %collective-permute-start.5 = (bf16[4,2,128,128]{3,2,1,0:T(8,128)(2,1)S(1)}, bf16[4,2,128,128]{3,2,1,0:T(8,128)(2,1)}, u32[]{:S(2)}, u32[]{:S(2)}) collective-permute-start(bf16[4,2,128,128]{3,2,1,0:T(8,128)(2,1)S(1)} %get-tuple-element.39), channel_id=1, source_target_pairs={{0,3},{1,0},{2,1},{3,2},{4,7},{5,4},{6,5},{7,6},{8,11},{9,8},{10,9... | collective-permute-start | bytes 786440 | tf_op jit(solution)/shard_map/ppermute | solution.py:442
  56.9 15.9 %all-to-all-start.2 = ((f32[16,36,128]{2,1,0:T(8,128)}), f32[16,36,128]{2,1,0:T(8,128)S(1)}, u32[]{:S(2)}, u32[]{:S(2)}) async-start(f32[16,36,128]{2,1,0:T(8,128)} %broadcast_in_dim.146), calls=%async_computation.2 | async-start | bytes 655360 | tf_op jit(solution)/shard_map/all_to_all | solution.py:541
  60.5 129.3 %all-gather.6.cloned.1.call-start = ((), (), s32[]{:S(2)}) async-start(), calls=%async_computation.6 | async-start | bytes 7077888 | tf_op jit(solution)/shard_map/all_gather | solution.py:550
  68.6 9.7 %collective-permute-start.8 = (bf16[2,2,128,128]{3,2,1,0:T(8,128)(2,1)}, bf16[2,2,128,128]{3,2,1,0:T(8,128)(2,1)}, u32[]{:S(2)}, u32[]{:S(2)}) collective-permute-start(bf16[2,2,128,128]{3,2,1,0:T(8,128)(2,1)} %get-tuple-element.92), channel_id=1, source_target_pairs={{0,12},{4,0},{8,4},{12,8},{1,13},{5,1},{9,5},{13,9},{2,14},{6,2},{... | collective-permute-start | bytes 393224 | tf_op jit(solution)/shard_map/ppermute | solution.py:442
  70.6 11.7 %collective-permute-start.6 = (bf16[2,2,128,128]{3,2,1,0:T(8,128)(2,1)}, bf16[2,2,128,128]{3,2,1,0:T(8,128)(2,1)}, u32[]{:S(2)}, u32[]{:S(2)}) collective-permute-start(bf16[2,2,128,128]{3,2,1,0:T(8,128)(2,1)} %get-tuple-element.94), channel_id=1, source_target_pairs={{0,4},{4,8},{8,12},{12,0},{1,5},{5,9},{9,13},{13,1},{2,6},{6,10},{... | collective-permute-start | bytes 393224 | tf_op jit(solution)/shard_map/ppermute | solution.py:442
  70.6 23.8 %copy-start.1 = (bf16[2048,512]{1,0:T(8,128)(2,1)S(1)}, bf16[2048,512]{1,0:T(8,128)(2,1)}, u32[]{:S(2)}) copy-start(bf16[2048,512]{1,0:T(8,128)(2,1)} %low.1) | copy-start | bytes 6291460
  70.6 18.9 %collective-permute-start.7 = (bf16[2,2,128,128]{3,2,1,0:T(8,128)(2,1)}, bf16[2,2,128,128]{3,2,1,0:T(8,128)(2,1)}, u32[]{:S(2)}, u32[]{:S(2)}) collective-permute-start(bf16[2,2,128,128]{3,2,1,0:T(8,128)(2,1)} %get-tuple-element.95), channel_id=1, source_target_pairs={{0,8},{4,12},{8,0},{12,4},{1,9},{5,13},{9,1},{13,5},{2,10},{6,14},... | collective-permute-start | bytes 393224 | tf_op jit(solution)/shard_map/ppermute | solution.py:442
  72.8 18.9 %collective-permute-start.2 = (f32[16,36,128]{2,1,0:T(8,128)S(1)}, f32[16,36,128]{2,1,0:T(8,128)S(1)}, u32[]{:S(2)}, u32[]{:S(2)}) collective-permute-start(f32[16,36,128]{2,1,0:T(8,128)S(1)} %all-to-all-done.2), channel_id=1, source_target_pairs={{0,96},{32,0},{64,32},{96,64},{1,97},{33,1},{65,33},{97,65},{2,98}... | collective-permute-start | bytes 884744 | tf_op jit(solution)/shard_map/ppermute | solution.py:442
  76.1 22.0 %collective-permute-start.1 = (f32[16,36,128]{2,1,0:T(8,128)S(1)}, f32[16,36,128]{2,1,0:T(8,128)}, u32[]{:S(2)}, u32[]{:S(2)}) collective-permute-start(f32[16,36,128]{2,1,0:T(8,128)S(1)} %all-to-all-done.2), channel_id=1, source_target_pairs={{0,64},{32,96},{64,0},{96,32},{1,65},{33,97},{65,1},{97,33},{2,66}... | collective-permute-start | bytes 884744 | tf_op jit(solution)/shard_map/ppermute | solution.py:442
  78.3 19.8 %collective-permute-start = (f32[16,36,128]{2,1,0:T(8,128)S(1)}, f32[16,36,128]{2,1,0:T(8,128)S(1)}, u32[]{:S(2)}, u32[]{:S(2)}) collective-permute-start(f32[16,36,128]{2,1,0:T(8,128)S(1)} %all-to-all-done.2), channel_id=1, source_target_pairs={{0,32},{32,64},{64,96},{96,0},{1,33},{33,65},{65,97},{97,1},{2,34}... | collective-permute-start | bytes 884744 | tf_op jit(solution)/shard_map/ppermute | solution.py:442
  82.3 15.9 %collective-permute-start.12 = (bf16[128,1024]{1,0:T(8,128)(2,1)}, bf16[128,1024]{1,0:T(8,128)(2,1)}, u32[]{:S(2)}, u32[]{:S(2)}) collective-permute-start(bf16[128,1024]{1,0:T(8,128)(2,1)} %get-tuple-element.86), channel_id=1, source_target_pairs={{0,96},{16,112},{1,97},{17,113},{2,98},{18,114},{3,99},{19,115},{3... | collective-permute-start | bytes 786440 | tf_op jit(solution)/shard_map/ppermute | solution.py:517
  89.5 8.6 %collective-permute-start.11 = (bf16[128,1024]{1,0:T(8,128)(2,1)S(1)}, bf16[128,1024]{1,0:T(8,128)(2,1)}, u32[]{:S(2)}, u32[]{:S(2)}) collective-permute-start(bf16[128,1024]{1,0:T(8,128)(2,1)S(1)} %get-tuple-element.87), channel_id=1, source_target_pairs={{0,64},{16,80},{1,65},{17,81},{2,66},{18,82},{3,67},{19,83},{36,10... | collective-permute-start | bytes 786440 | tf_op jit(solution)/shard_map/ppermute | solution.py:517
  92.5 8.7 %collective-permute-start.10 = (bf16[128,1024]{1,0:T(8,128)(2,1)S(1)}, bf16[128,1024]{1,0:T(8,128)(2,1)}, u32[]{:S(2)}, u32[]{:S(2)}) collective-permute-start(bf16[128,1024]{1,0:T(8,128)(2,1)S(1)} %get-tuple-element.88), channel_id=1, source_target_pairs={{0,32},{16,48},{1,33},{17,49},{2,34},{18,50},{3,35},{19,51},{36,68... | collective-permute-start | bytes 786440 | tf_op jit(solution)/shard_map/ppermute | solution.py:517
  109.3 9.5 %collective-permute-start.13 = (f32[4,16,36,128]{3,1,2,0:T(8,128)}, f32[4,16,36,128]{3,1,2,0:T(8,128)}, u32[]{:S(2)}, u32[]{:S(2)}) collective-permute-start(f32[4,16,36,128]{3,1,2,0:T(8,128)} %copy.73), channel_id=1, source_target_pairs={{0,16},{16,0},{1,17},{17,1},{2,18},{18,2},{3,19},{19,3},{4,20},{20... | collective-permute-start | bytes 3538952 | tf_op jit(solution)/shard_map/ppermute | solution.py:446
  112.0 39.4 %all-to-all-start.3 = ((bf16[32,4,64,128]{3,2,1,0:T(8,128)(2,1)}), bf16[32,4,64,128]{3,2,1,0:T(8,128)(2,1)S(1)}, u32[]{:S(2)}, u32[]{:S(2)}) async-start(bf16[32,4,64,128]{3,2,1,0:T(8,128)(2,1)} %pack_rows.1), calls=%async_computation.3 | async-start | bytes 4194304 | tf_op jit(solution)/shard_map/all_to_all | solution.py:546
  154.7 8.0 %copy-start.3 = (f32[4,2,16,36,128]{4,2,1,0,3:T(8,128)S(1)}, f32[4,2,16,36,128]{4,2,1,0,3:T(8,128)}, u32[]{:S(2)}) copy-start(f32[4,2,16,36,128]{4,2,1,0,3:T(8,128)} %copy-done.2) | copy-start | bytes 7077892
  154.7 69.9 %all-to-all-start.4 = ((bf16[16,8,2,64,128]{4,3,2,1,0:T(8,128)(2,1)}), bf16[16,8,2,64,128]{4,3,2,1,0:T(8,128)(2,1)}, u32[]{:S(2)}, u32[]{:S(2)}) async-start(bf16[16,8,2,64,128]{4,3,2,1,0:T(8,128)(2,1)} %copy-done), calls=%async_computation.4 | async-start | bytes 8388608 | tf_op jit(solution)/shard_map/all_to_all | solution.py:562
  (12 other events, 22.0 us)
Sparse Core Ops, SparseCore 0:
  34.6 60.7 all-gather.3
  104.8 64.3 all-gather.5
